TPU v7x, 256 devices: a whole 4x4x8 slice. The times are simulated.
256 devices in a mesh: ctx: 32 (over x, z), head: 8 (over y, core).
Axes of the slice: x: 4, y: 4, z: 8, core: 2. Of those that a mesh axis runs over, the one named last changes fastest.
Arguments:
- query: bfloat16 [65536, 8192], P(('ctx', 'head')), as said below
- key: bfloat16 [65536, 1024], P(('ctx', 'head')), as said below
- value: bfloat16 [65536, 1024], P(('ctx', 'head')), may hold values from -6 to 6
- doc_ids: int32 [512], replicated, may hold values from 0 to 84, never falling along the last dimension, each value on 1 to 8 neighbouring positions
- plan: int32 [512], replicated, may hold values from 0 to 511, as said below
Outputs:
- attended: bfloat16 [65536, 8192], P('ctx', 'head')
Inputs may be any that keep to these rules, and one draw needn't show every extreme that they name: `doc_ids`: block ids never fall; each document holds 1 to 8 blocks, one exactly 8. `plan`: A permutation of the 512 blocks. Output positions k * 16 to (k + 1) * 16 - 1 belong to context shard k. Every shard receives 16 blocks; of the blocks j * 16 to (j + 1) * 16 - 1 at most 1 go to one shard, and exactly 1 to some shard. `query`: real values; no structure promised. `key`: real values; no structure promised.
All inputs are finite; a program needn't handle non-finite values.
Results may differ from a plain program's by a relative error of at most 0.0038.
Values may be sent and summed in bfloat16 or wider, within the bound.
No kernel may reach another device: no remote copies, remote signals or barrier semaphores. Data moves between devices by JAX's collectives and lax.ppermute only.
A program may use at most 128 MiB of HBM per device.

v0:
```python
import math

import jax
import jax.numpy as jnp
from jax import lax
from jax.sharding import PartitionSpec as P

HD = 128
BLK = 128
MAXDOC = 8


def shifted(shard, axis, by):
    count = lax.axis_size(axis)
    pairs = [(i, i + by) for i in range(count) if 0 <= i + by < count]
    return lax.ppermute(shard, axis, pairs)


def attend(query_set, block_ids, keys_all, values_all, first_block, doc_start, kv_heads, group):
    count = query_set.shape[0]
    q_width = query_set.shape[2]
    scale = 1.0 / math.sqrt(HD)
    positions = jnp.arange(BLK, dtype=jnp.int32)
    causal = positions[None, :] <= positions[:, None]

    def per_block(index, result):
        block = block_ids[index]
        begin = doc_start[block]
        queries = lax.dynamic_index_in_dim(query_set, index, 0, False).reshape(
            BLK, kv_heads, group, HD
        )

        def per_tile(tile, carry):
            running, total, accum = carry
            keys = lax.dynamic_index_in_dim(keys_all, tile - first_block, 0, False).reshape(
                BLK, kv_heads, HD
            )
            values = lax.dynamic_index_in_dim(values_all, tile - first_block, 0, False).reshape(
                BLK, kv_heads, HD
            )
            scores = (
                jnp.einsum("qkgd,skd->kgqs", queries, keys, preferred_element_type=jnp.float32)
                * scale
            )
            allowed = causal | (tile < block)
            scores = jnp.where(allowed, scores, -jnp.inf)
            highest = jnp.maximum(running, jnp.max(scores, axis=3))
            factor = jnp.exp(running - highest)
            expo = jnp.exp(scores - highest[..., None])
            total = total * factor + jnp.sum(expo, axis=3)
            accum = accum * factor[..., None] + jnp.einsum(
                "kgqs,skd->kgqd",
                expo.astype(jnp.bfloat16),
                values,
                preferred_element_type=jnp.float32,
            )
            return (highest, total, accum)

        start_state = (
            jnp.full((kv_heads, group, BLK), -jnp.inf, jnp.float32),
            jnp.zeros((kv_heads, group, BLK), jnp.float32),
            jnp.zeros((kv_heads, group, BLK, HD), jnp.float32),
        )
        _, total, accum = lax.fori_loop(begin, block + 1, per_tile, start_state)
        mixed = (
            (accum / total[..., None])
            .transpose(2, 0, 1, 3)
            .reshape(BLK, q_width)
            .astype(jnp.bfloat16)
        )
        return lax.dynamic_update_index_in_dim(result, mixed, index, 0)

    return lax.fori_loop(0, count, per_block, jnp.zeros((count, BLK, q_width), jnp.bfloat16))


def shards(query, key, value, doc_ids, plan):
    head_count = lax.axis_size("head")
    shard_count = lax.axis_size("ctx")
    local_rows = query.shape[0]
    q_parts = query.reshape(local_rows, head_count, query.shape[1] // head_count)
    k_parts = key.reshape(local_rows, head_count, key.shape[1] // head_count)
    v_parts = value.reshape(local_rows, head_count, value.shape[1] // head_count)
    q_heads, k_heads, v_heads = (
        lax.all_to_all(q_parts, "head", split_axis=1, concat_axis=0, tiled=True),
        lax.all_to_all(k_parts, "head", split_axis=1, concat_axis=0, tiled=True),
        lax.all_to_all(v_parts, "head", split_axis=1, concat_axis=0, tiled=True),
    )
    blocks_here = head_count * local_rows // BLK
    q_width = q_heads.shape[2]
    kv_width = k_heads.shape[2]
    kv_heads = kv_width // HD
    group = q_width // HD // kv_heads
    q_blocks = q_heads.reshape(blocks_here, BLK, q_width)
    k_blocks = k_heads.reshape(blocks_here, BLK, kv_width)
    v_blocks = v_heads.reshape(blocks_here, BLK, kv_width)
    shard = lax.axis_index("ctx")
    total_blocks = doc_ids.shape[0]
    block_iota = jnp.arange(total_blocks, dtype=jnp.int32)
    doc_start = jnp.sum((doc_ids[None, :] < doc_ids[:, None]).astype(jnp.int32), axis=1)
    position = jnp.zeros((total_blocks,), jnp.int32).at[plan].set(block_iota)
    target = position // blocks_here
    target_grid = target.reshape(shard_count, blocks_here)
    local_iota = jnp.arange(blocks_here, dtype=jnp.int32)
    lower = local_iota[None, :] < local_iota[:, None]
    same_before = (target_grid[:, :, None] == target_grid[:, None, :]) & lower[None, :, :]
    rank = jnp.sum(same_before.astype(jnp.int32), axis=2).reshape(total_blocks)
    capacity = -(-blocks_here // shard_count)
    slots = shard_count * capacity
    slot_iota = jnp.arange(slots, dtype=jnp.int32)
    own_ids = shard * blocks_here + local_iota
    plan_ids = lax.dynamic_slice_in_dim(plan, shard * blocks_here, blocks_here)
    depth = (MAXDOC - 2 + blocks_here) // blocks_here
    stacked = jnp.stack([k_blocks, v_blocks])
    pieces = []
    pieces.append(shifted(stacked, "ctx", 1))
    pieces.append(stacked)
    window = jnp.concatenate(pieces, axis=1)
    local_out = attend(
        q_blocks,
        own_ids,
        window[0],
        window[1],
        (shard - depth) * blocks_here,
        doc_start,
        kv_heads,
        group,
    )
    slot = target[own_ids] * capacity + rank[own_ids]
    select = (slot_iota[:, None] == slot[None, :]).astype(jnp.bfloat16)
    flat = local_out.reshape(blocks_here, BLK * q_width)
    received = lax.all_to_all(
        jnp.dot(select, flat, preferred_element_type=jnp.bfloat16).reshape(slots, BLK, q_width),
        "ctx",
        split_axis=0,
        concat_axis=0,
        tiled=True,
    )
    slot = plan_ids // blocks_here * capacity + rank[plan_ids]
    select = (slot[:, None] == slot_iota[None, :]).astype(jnp.bfloat16)
    flat = received.reshape(slots, BLK * q_width)
    result = jnp.dot(select, flat, preferred_element_type=jnp.bfloat16).reshape(
        blocks_here, BLK, q_width
    )
    return result.reshape(blocks_here * BLK, q_width)


def solution(mesh):
    return jax.shard_map(
        shards,
        mesh=mesh,
        in_specs=(
            P(("ctx", "head"), None),
            P(("ctx", "head"), None),
            P(("ctx", "head"), None),
            P(),
            P(),
        ),
        out_specs=P("ctx", "head"),
        check_vma=False,
    )
```

profile of v0, /device:TPU:33, one launch (start us, length us, event | category | flops | bytes accessed | tf_op | source)
XLA Modules:
  0.0 687.5 jit_solution(11976684673824803982)
XLA Ops:
  0.0 1.0 copy-done
  1.9 5.1 all-to-all-start.1
  7.1 1.9 copy_bitcast_fusion
  9.0 7.6 %all-to-all-done.1 = bf16[256,8,128]{2,0,1:T(8,128)(2,1)S(1)} async-done(((bf16[256,8,128]{2,0,1:T(8,128)(2,1)}), bf16[256,8,128]{2,0,1:T(8,128)(2,1)S(1)}, u32[]{:S(2)}, u32[]{:S(2)}) %all-to-all-start.1) | async-done | bytes 524320 | tf_op jit(solution)/shard_map/all_to_all | solution.py:85
  16.6 4.3 all-to-all-start.2
  20.8 6.4 copy.52
  27.2 3.1 all-to-all-done.2
  30.3 5.5 all-to-all-start
  35.9 3.5 collective-permute-start
  39.5 2.6 scatter_custom_fusion
  44.2 18.3 %collective-permute-done = bf16[2,16,128,128]{3,2,1,0:T(8,128)(2,1)} collective-permute-done((bf16[2,16,128,128]{3,2,1,0:T(8,128)(2,1)S(1)}, bf16[2,16,128,128]{3,2,1,0:T(8,128)(2,1)}, u32[]{:S(2)}, u32[]{:S(2)}) %collective-permute-start) | collective-permute-done | bytes 1048608 | tf_op jit(solution)/shard_map/ppermute | solution.py:16
  62.5 1.4 maximum_maximum_fusion
  64.1 20.6 %all-to-all-done = bf16[256,8,1024]{0,2,1:T(8,128)(2,1)} async-done(((bf16[256,8,1024]{0,2,1:T(8,128)(2,1)}), bf16[256,8,1024]{0,2,1:T(8,128)(2,1)}, u32[]{:S(2)}, u32[]{:S(2)}) %all-to-all-start) | async-done | bytes 4194336 | tf_op jit(solution)/shard_map/all_to_all | solution.py:84
  84.7 6.5 copy.53
  91.2 304.8 %while.46 = (s32[]{:T(128)}, bf16[16,128,1024]{2,1,0:T(8,128)(2,1)}, s32[16]{0:T(128)S(1)}, s32[512]{0:T(512)S(1)}, bf16[16,128,1024]{2,1,0:T(8,128)(2,1)}, /*in...) while((s32[]{:T(128)}, ...), condition=%wide.region_8.9_spmd.clone, body=%wide.region_3.8_spmd.clone.sunk | while | flops 68586512 | bytes 7549492 | solution.py:73
  95.2 1.0 constant_dynamic-slice_fusion.2
  96.6 17.1 %while.47 = (s32[]{:T(128)}, f32[1,8,128]{2,1,0:T(8,128)S(1)}, f32[1,8,128]{2,1,0:T(8,128)S(1)}, f32[1,8,128,128]{3,2,1,0:T(8,128)S(1)}, s32[]{:T(128)}, /*index...) while((s32[]{:T(128)}, f32[1,8,128]{2,1,0:T(8,128)S(1)}, ...), condition=%wide.region_7.7_spmd, body=%wide.region_4.6_spmd.sunk | while | flops 68307976 | bytes 3064013 | solution.py:64
  119.0 1.0 constant_dynamic-slice_fusion.2
  120.4 20.4 %while.47 = (s32[]{:T(128)}, f32[1,8,128]{2,1,0:T(8,128)S(1)}, f32[1,8,128]{2,1,0:T(8,128)S(1)}, f32[1,8,128,128]{3,2,1,0:T(8,128)S(1)}, s32[]{:T(128)}, /*index...) while((s32[]{:T(128)}, f32[1,8,128]{2,1,0:T(8,128)S(1)}, ...), condition=%wide.region_7.7_spmd, body=%wide.region_4.6_spmd.sunk | while | flops 68307976 | bytes 3064013 | solution.py:64
  146.1 1.0 constant_dynamic-slice_fusion.2
  147.5 3.9 while.47
  156.7 1.0 constant_dynamic-slice_fusion.2
  158.1 3.9 while.47
  168.7 7.2 %while.47 = (s32[]{:T(128)}, f32[1,8,128]{2,1,0:T(8,128)S(1)}, f32[1,8,128]{2,1,0:T(8,128)S(1)}, f32[1,8,128,128]{3,2,1,0:T(8,128)S(1)}, s32[]{:T(128)}, /*index...) while((s32[]{:T(128)}, f32[1,8,128]{2,1,0:T(8,128)S(1)}, ...), condition=%wide.region_7.7_spmd, body=%wide.region_4.6_spmd.sunk | while | flops 68307976 | bytes 3064013 | solution.py:64
  181.2 1.0 constant_dynamic-slice_fusion.2
  182.6 3.9 while.47
  191.8 1.0 constant_dynamic-slice_fusion.2
  193.2 7.2 %while.47 = (s32[]{:T(128)}, f32[1,8,128]{2,1,0:T(8,128)S(1)}, f32[1,8,128]{2,1,0:T(8,128)S(1)}, f32[1,8,128,128]{3,2,1,0:T(8,128)S(1)}, s32[]{:T(128)}, /*index...) while((s32[]{:T(128)}, f32[1,8,128]{2,1,0:T(8,128)S(1)}, ...), condition=%wide.region_7.7_spmd, body=%wide.region_4.6_spmd.sunk | while | flops 68307976 | bytes 3064013 | solution.py:64
  207.1 10.5 %while.47 = (s32[]{:T(128)}, f32[1,8,128]{2,1,0:T(8,128)S(1)}, f32[1,8,128]{2,1,0:T(8,128)S(1)}, f32[1,8,128,128]{3,2,1,0:T(8,128)S(1)}, s32[]{:T(128)}, /*index...) while((s32[]{:T(128)}, f32[1,8,128]{2,1,0:T(8,128)S(1)}, ...), condition=%wide.region_7.7_spmd, body=%wide.region_4.6_spmd.sunk | while | flops 68307976 | bytes 3064013 | solution.py:64
  222.9 1.0 constant_dynamic-slice_fusion.2
  224.3 13.8 %while.47 = (s32[]{:T(128)}, f32[1,8,128]{2,1,0:T(8,128)S(1)}, f32[1,8,128]{2,1,0:T(8,128)S(1)}, f32[1,8,128,128]{3,2,1,0:T(8,128)S(1)}, s32[]{:T(128)}, /*index...) while((s32[]{:T(128)}, f32[1,8,128]{2,1,0:T(8,128)S(1)}, ...), condition=%wide.region_7.7_spmd, body=%wide.region_4.6_spmd.sunk | while | flops 68307976 | bytes 3064013 | solution.py:64
  244.8 17.1 %while.47 = (s32[]{:T(128)}, f32[1,8,128]{2,1,0:T(8,128)S(1)}, f32[1,8,128]{2,1,0:T(8,128)S(1)}, f32[1,8,128,128]{3,2,1,0:T(8,128)S(1)}, s32[]{:T(128)}, /*index...) while((s32[]{:T(128)}, f32[1,8,128]{2,1,0:T(8,128)S(1)}, ...), condition=%wide.region_7.7_spmd, body=%wide.region_4.6_spmd.sunk | while | flops 68307976 | bytes 3064013 | solution.py:64
  268.6 20.4 %while.47 = (s32[]{:T(128)}, f32[1,8,128]{2,1,0:T(8,128)S(1)}, f32[1,8,128]{2,1,0:T(8,128)S(1)}, f32[1,8,128,128]{3,2,1,0:T(8,128)S(1)}, s32[]{:T(128)}, /*index...) while((s32[]{:T(128)}, f32[1,8,128]{2,1,0:T(8,128)S(1)}, ...), condition=%wide.region_7.7_spmd, body=%wide.region_4.6_spmd.sunk | while | flops 68307976 | bytes 3064013 | solution.py:64
  294.2 1.0 constant_dynamic-slice_fusion.2
  295.7 23.7 %while.47 = (s32[]{:T(128)}, f32[1,8,128]{2,1,0:T(8,128)S(1)}, f32[1,8,128]{2,1,0:T(8,128)S(1)}, f32[1,8,128,128]{3,2,1,0:T(8,128)S(1)}, s32[]{:T(128)}, /*index...) while((s32[]{:T(128)}, f32[1,8,128]{2,1,0:T(8,128)S(1)}, ...), condition=%wide.region_7.7_spmd, body=%wide.region_4.6_spmd.sunk | while | flops 68307976 | bytes 3064013 | solution.py:64
  324.6 1.0 constant_dynamic-slice_fusion.2
  326.1 27.0 %while.47 = (s32[]{:T(128)}, f32[1,8,128]{2,1,0:T(8,128)S(1)}, f32[1,8,128]{2,1,0:T(8,128)S(1)}, f32[1,8,128,128]{3,2,1,0:T(8,128)S(1)}, s32[]{:T(128)}, /*index...) while((s32[]{:T(128)}, f32[1,8,128]{2,1,0:T(8,128)S(1)}, ...), condition=%wide.region_7.7_spmd, body=%wide.region_4.6_spmd.sunk | while | flops 68307976 | bytes 3064013 | solution.py:64
  359.8 3.9 while.47
  370.4 7.2 %while.47 = (s32[]{:T(128)}, f32[1,8,128]{2,1,0:T(8,128)S(1)}, f32[1,8,128]{2,1,0:T(8,128)S(1)}, f32[1,8,128,128]{3,2,1,0:T(8,128)S(1)}, s32[]{:T(128)}, /*index...) while((s32[]{:T(128)}, f32[1,8,128]{2,1,0:T(8,128)S(1)}, ...), condition=%wide.region_7.7_spmd, body=%wide.region_4.6_spmd.sunk | while | flops 68307976 | bytes 3064013 | solution.py:64
  382.8 1.0 constant_dynamic-slice_fusion.2
  384.3 10.5 %while.47 = (s32[]{:T(128)}, f32[1,8,128]{2,1,0:T(8,128)S(1)}, f32[1,8,128]{2,1,0:T(8,128)S(1)}, f32[1,8,128,128]{3,2,1,0:T(8,128)S(1)}, s32[]{:T(128)}, /*index...) while((s32[]{:T(128)}, f32[1,8,128]{2,1,0:T(8,128)S(1)}, ...), condition=%wide.region_7.7_spmd, body=%wide.region_4.6_spmd.sunk | while | flops 68307976 | bytes 3064013 | solution.py:64
  396.0 8.8 %fusion.19 = bf16[32,128,1024]{2,0,1:T(8,128)(2,1)} fusion(s32[16]{0:T(128)S(1)} %add.114, bf16[2,8,128,1024]{3,2,1,0:T(8,128)(2,1)} %bitcast.132), kind=kOutput, calls=%fused_computation.32 | convolution fusion | flops 134218240 | bytes 12582976 | tf_op jit(solution)/shard_map/dot_general | solution.py:132
  404.8 11.3 %copy.58 = bf16[32,128,1024]{2,1,0:T(8,128)(2,1)} copy(bf16[32,128,1024]{2,0,1:T(8,128)(2,1)} %fusion.19) | data formatting | bytes 16777216 | tf_op jit(solution)/shard_map/dot_general | solution.py:132
  416.1 59.3 %all-to-all-start.3 = ((bf16[32,128,1024]{2,1,0:T(8,128)(2,1)}), bf16[32,128,1024]{2,1,0:T(8,128)(2,1)}, u32[]{:S(2)}, u32[]{:S(2)}) async-start(bf16[32,128,1024]{2,1,0:T(8,128)(2,1)} %copy.58), calls=%async_computation.3 | async-start | bytes 16777216 | tf_op jit(solution)/shard_map/all_to_all | solution.py:131
  476.3 188.3 %all-to-all-done.3 = bf16[32,128,1024]{2,1,0:T(8,128)(2,1)} async-done(((bf16[32,128,1024]{2,1,0:T(8,128)(2,1)}), bf16[32,128,1024]{2,1,0:T(8,128)(2,1)}, u32[]{:S(2)}, u32[]{:S(2)}) %all-to-all-start.3) | async-done | bytes 8388640 | tf_op jit(solution)/shard_map/all_to_all | solution.py:131
  664.6 11.4 %copy.65 = bf16[4,8,128,1024]{3,1,2,0:T(8,128)(2,1)} copy(bf16[4,8,128,1024]{3,2,1,0:T(8,128)(2,1)} %bitcast.49) | data formatting | bytes 16777216
  676.0 6.7 fusion.22
  682.7 4.8 reshape_reshape.3
  (628 shorter events, 102.1 us)
Async XLA Ops:
  0.0 1.0 copy-start
  1.9 14.6 %all-to-all-start.1 = ((bf16[256,8,128]{2,0,1:T(8,128)(2,1)}), bf16[256,8,128]{2,0,1:T(8,128)(2,1)S(1)}, u32[]{:S(2)}, u32[]{:S(2)}) async-start(bf16[256,8,128]{2,0,1:T(8,128)(2,1)} %copy_bitcast_fusion.1), calls=%async_computation.1 | async-start | bytes 1048576 | tf_op jit(solution)/shard_map/all_to_all | solution.py:85
  16.6 13.8 %all-to-all-start.2 = ((bf16[256,8,128]{2,0,1:T(8,128)(2,1)}), bf16[256,8,128]{2,0,1:T(8,128)(2,1)S(1)}, u32[]{:S(2)}, u32[]{:S(2)}) async-start(bf16[256,8,128]{2,0,1:T(8,128)(2,1)} %copy_bitcast_fusion), calls=%async_computation.2 | async-start | bytes 1048576 | tf_op jit(solution)/shard_map/all_to_all | solution.py:86
  30.3 9.1 %copy-start.3 = (s32[512]{0:T(512)S(1)}, s32[512]{0:T(512)}, u32[]{:S(2)}) copy-start(s32[512]{0:T(512)} %param.13) | copy-start | bytes 6148
  30.3 13.6 %copy-start.2 = (s32[512]{0:T(512)S(1)}, s32[512]{0:T(512)}, u32[]{:S(2)}) copy-start(s32[512]{0:T(512)} %param.12) | copy-start | bytes 6148
  30.3 54.4 %all-to-all-start = ((bf16[256,8,1024]{0,2,1:T(8,128)(2,1)}), bf16[256,8,1024]{0,2,1:T(8,128)(2,1)}, u32[]{:S(2)}, u32[]{:S(2)}) async-start(bf16[256,8,1024]{0,2,1:T(8,128)(2,1)} %bitcast.125), calls=%async_computation | async-start | bytes 8388608 | tf_op jit(solution)/shard_map/all_to_all | solution.py:84
  35.9 26.6 %collective-permute-start = (bf16[2,16,128,128]{3,2,1,0:T(8,128)(2,1)S(1)}, bf16[2,16,128,128]{3,2,1,0:T(8,128)(2,1)}, u32[]{:S(2)}, u32[]{:S(2)}) collective-permute-start(bf16[2,16,128,128]{3,2,1,0:T(8,128)(2,1)S(1)} %pad_maximum_fusion), channel_id=1, source_target_pairs={{0,8},{8,16},{16,24},{24,32},{32,40},{40,48},{48,56},{56,64},{64,7... | collective-permute-start | bytes 3145736 | tf_op jit(solution)/shard_map/ppermute | solution.py:16
  416.1 248.5 %all-to-all-start.3 = ((bf16[32,128,1024]{2,1,0:T(8,128)(2,1)}), bf16[32,128,1024]{2,1,0:T(8,128)(2,1)}, u32[]{:S(2)}, u32[]{:S(2)}) async-start(bf16[32,128,1024]{2,1,0:T(8,128)(2,1)} %copy.58), calls=%async_computation.3 | async-start | bytes 16777216 | tf_op jit(solution)/shard_map/all_to_all | solution.py:131
  676.0 11.5 %copy-start.1 = (bf16[256,1024]{1,0:T(8,128)(2,1)S(1)}, bf16[256,1024]{1,0:T(8,128)(2,1)}, u32[]{:S(2)}) copy-start(bf16[256,1024]{1,0:T(8,128)(2,1)} %param.10) | copy-start | bytes 1572868
where the time goes:
time: 694 us; the launch traced here: 687 us
  waiting for transfers between devices  238 us (34%)
  loops' own time  197 us (28%)
  local copies, waits for them, and re-layouts  108 us (16%)
  starting transfers between devices  77.7 us (11%)
  matrix products  54.1 us (8%)
  other arithmetic  12.4 us (2%)
    all_to_all x1, waiting for transfers between devices, shards(): lax.all_to_all(jnp.dot(select, flat, preferred_element_type=jnp.bfloat16)...  188 us
    another operation x16, loops' own time, per_block(): _, total, accum = lax.fori_loop(begin, block + 1, per_tile, start_state)  152 us
    all_to_all x1, starting transfers between devices, shards(): lax.all_to_all(jnp.dot(select, flat, preferred_element_type=jnp.bfloat16)...  59.3 us
    another operation x1, loops' own time, attend(): lax.fori_loop(0, count, per_block, jnp.zeros((count, BLK, q_width), jnp.b...  44.7 us
    dot_general x57, matrix products, per_tile(): jnp.einsum('kgqs,skd->kgqd', expo.astype(jnp.bfloat16), values, preferred...  24.9 us
    all_to_all x1, waiting for transfers between devices, shards(): lax.all_to_all(q_parts, 'head', split_axis=1, concat_axis=0, tiled=True)  20.6 us
    unnamed x10, local copies, waits for them, and re-layouts  18.8 us
    ppermute x1, waiting for transfers between devices, shifted(): return lax.ppermute(shard, axis, pairs)  18.3 us
  transfers between devices with their start and end apart: 5, of which 5 were waited for; matrix products, arithmetic and copies ran while one was open for 2% of the time, Pallas kernels for 0%

commit v1 on v0

v1 whole, which is shorter than its diff:
```python
import functools
import math

import jax
import jax.numpy as jnp
from jax import lax
from jax.experimental import pallas as pl
from jax.experimental.pallas import tpu as pltpu
from jax.sharding import PartitionSpec as P

HD = 128
BLK = 128
MAXDOC = 8
HALO = MAXDOC - 1
CHUNKS = (2, 2, 2, 2)
EXP2_SCALE = math.log2(math.e) / math.sqrt(HD)


def attend_kernel(doc_ref, slot_ref, shard_ref, q_ref, own_ref, halo_ref, out_ref, win_ref, *, heads, count):
    index = pl.program_id(0)

    @pl.when(index == 0)
    def _():
        win_ref[: HALO * BLK, :] = halo_ref[...]
        win_ref[HALO * BLK :, :] = own_ref[...]

    block = shard_ref[0] * count + index
    doc = doc_ref[block]
    tiles = jnp.int32(1)
    for back in range(1, MAXDOC):
        at = jnp.maximum(block - back, 0)
        tiles += jnp.where((block >= back) & (doc_ref[at] == doc), 1, 0)

    row = lax.broadcasted_iota(jnp.int32, (BLK, BLK), 0)
    column = lax.broadcasted_iota(jnp.int32, (BLK, BLK), 1)
    causal = column <= row

    def with_tiles(n):
        start = pl.multiple_of((index + MAXDOC - n) * BLK, BLK)
        keys = win_ref[pl.ds(start, n * BLK), :HD]
        values = win_ref[pl.ds(start, n * BLK), HD:]
        for head in range(heads):
            columns = slice(head * HD, (head + 1) * HD)
            scores = lax.dot_general(
                q_ref[:, columns], keys, (((1,), (1,)), ((), ())), preferred_element_type=jnp.float32
            )
            last = jnp.where(causal, scores[:, (n - 1) * BLK :], -jnp.inf)
            if n > 1:
                scores = jnp.concatenate([scores[:, : (n - 1) * BLK], last], axis=1)
            else:
                scores = last
            top = jnp.max(scores, axis=1, keepdims=True)
            expo = jnp.exp2((scores - top) * EXP2_SCALE)
            total = jnp.sum(expo, axis=1, keepdims=True)
            mixed = jnp.dot(expo.astype(jnp.bfloat16), values, preferred_element_type=jnp.float32)
            out_ref[0, :, columns] = (mixed / total).astype(jnp.bfloat16)

    for n in range(1, MAXDOC + 1):
        pl.when(tiles == n)(functools.partial(with_tiles, n))


def attend(queries, kv_own, kv_halo, doc_ids, slot, shard, slots):
    rows, width = queries.shape
    count = rows // BLK
    heads = width // HD
    return pl.pallas_call(
        functools.partial(attend_kernel, heads=heads, count=count),
        grid_spec=pltpu.PrefetchScalarGridSpec(
            num_scalar_prefetch=3,
            grid=(count,),
            in_specs=[
                pl.BlockSpec((BLK, width), lambda i, doc, slot, shard: (i, 0)),
                pl.BlockSpec(kv_own.shape, lambda i, doc, slot, shard: (0, 0)),
                pl.BlockSpec(kv_halo.shape, lambda i, doc, slot, shard: (0, 0)),
            ],
            out_specs=pl.BlockSpec((1, BLK, width), lambda i, doc, slot, shard: (slot[i], 0, 0)),
            scratch_shapes=[pltpu.VMEM((kv_own.shape[0] + kv_halo.shape[0], 2 * HD), jnp.bfloat16)],
        ),
        out_shape=jax.ShapeDtypeStruct((slots, BLK, width), jnp.bfloat16),
        compiler_params=pltpu.CompilerParams(vmem_limit_bytes=32 * 1024 * 1024),
        cost_estimate=pl.CostEstimate(
            flops=4 * rows * heads * HD * BLK * 4,
            bytes_accessed=4 * rows * width + 4 * kv_own.size,
            transcendentals=rows * heads * BLK * 4,
        ),
        name="attend",
    )(doc_ids, slot, shard, queries, kv_own, kv_halo)


def place_kernel(source_ref, *refs, count, first, width):
    received_ref, out_ref, sems = refs[0], refs[-2], refs[-1]

    def copy(i):
        return pltpu.make_async_copy(
            received_ref.at[source_ref[i]],
            out_ref.at[pl.ds(i * BLK, BLK), pl.ds(first, width)],
            sems.at[i],
        )

    for i in range(count):
        copy(i).start()
    for i in range(count):
        copy(i).wait()


def place(received, source, result, first, count, full_width):
    slots, _, width = received.shape
    given = [received] if result is None else [received, result]
    return pl.pallas_call(
        functools.partial(place_kernel, count=count, first=first, width=width),
        in_specs=[pl.BlockSpec(memory_space=pltpu.SMEM)] + [pl.BlockSpec(memory_space=pl.ANY)] * len(given),
        out_specs=pl.BlockSpec(memory_space=pl.ANY),
        out_shape=jax.ShapeDtypeStruct((count * BLK, full_width), jnp.bfloat16),
        scratch_shapes=[pltpu.SemaphoreType.DMA((count,))],
        input_output_aliases={} if result is None else {2: 0},
        cost_estimate=pl.CostEstimate(flops=0, bytes_accessed=4 * count * BLK * width, transcendentals=0),
        name="place",
    )(source, *given)


def shards(query, key, value, doc_ids, plan):
    head_count = lax.axis_size("head")
    shard_count = lax.axis_size("ctx")
    local_rows = query.shape[0]
    rows = head_count * local_rows
    count = rows // BLK
    q_width = query.shape[1] // head_count
    shard = lax.axis_index("ctx").astype(jnp.int32)

    def to_heads(parts):
        moved = lax.all_to_all(parts.transpose(1, 0, 2), "head", split_axis=0, concat_axis=0, tiled=True)
        return moved.reshape(rows, parts.shape[2])

    kv_parts = jnp.concatenate(
        [key.reshape(local_rows, head_count, HD), value.reshape(local_rows, head_count, HD)], axis=2
    )
    kv_own = to_heads(kv_parts)
    kv_halo = lax.ppermute(
        kv_own[rows - HALO * BLK :], "ctx", [(i, i + 1) for i in range(shard_count - 1)]
    )

    own_ids = shard * count + jnp.arange(count, dtype=jnp.int32)
    position = jnp.arange(plan.shape[0], dtype=jnp.int32)
    target = jnp.sum(
        jnp.where(plan[None, :] == own_ids[:, None], position[None, :] // count, 0), axis=1, dtype=jnp.int32
    )
    source = lax.dynamic_slice_in_dim(plan, shard * count, count) // count

    q_parts = query.reshape(local_rows, head_count, q_width)
    result = None
    first = 0
    for heads in CHUNKS:
        width = heads * HD
        queries = to_heads(q_parts[:, :, first : first + width])
        sent = attend(queries, kv_own, kv_halo, doc_ids, target, shard.reshape(1), shard_count)
        received = lax.all_to_all(sent, "ctx", split_axis=0, concat_axis=0, tiled=True)
        result = place(received, source, result, first, count, q_width)
        first += width
    return result


def solution(mesh):
    return jax.shard_map(
        shards,
        mesh=mesh,
        in_specs=(
            P(("ctx", "head"), None),
            P(("ctx", "head"), None),
            P(("ctx", "head"), None),
            P(),
            P(),
        ),
        out_specs=P("ctx", "head"),
        check_vma=False,
    )
```

time: 694 us -> 437 us (0.63)
  loops' own time: 197 us -> 0 us
  Pallas kernels: 0 us -> 190 us
  local copies, waits for them, and re-layouts: 108 us -> 24.5 us
  waiting for transfers between devices: 238 us -> 155 us
  matrix products: 54.1 us -> 0 us
  starting transfers between devices: 77.7 us -> 59.5 us
  other arithmetic: 12.4 us -> 1.98 us
    another operation x17 -> x0, loops' own time: 197 us -> none  [the longest x16 152 us: per_block(): _, total, accum = lax.fori_loop(begin, block + 1, per_tile, start_state)]
    pallas_call x0 -> x8, Pallas kernels: none -> 190 us  [the longest x4 135 us: place(): pl.pallas_call(functools.partial(place_kernel, count=count, first=first,...]
    all_to_all x4 -> x9, waiting for transfers between devices: 220 us -> 145 us  [the longest x4 101 us: shards(): lax.all_to_all(sent, 'ctx', split_axis=0, concat_axis=0, tiled=True)]
    dot_general x116 -> x0, matrix products: 54.1 us -> none  [the longest x57 24.9 us: per_tile(): jnp.einsum('kgqs,skd->kgqd', expo.astype(jnp.bfloat16), values, preferred...]
    dynamic_slice x64 -> x0, local copies, waits for them, and re-layouts: 38.5 us -> none  [the longest x32 18.3 us: per_block(): lax.dynamic_index_in_dim(query_set, index, 0, False)]
    all_to_all x4 -> x9, starting transfers between devices: 74.2 us -> 56 us  [the longest x4 31.6 us: shards(): lax.all_to_all(sent, 'ctx', split_axis=0, concat_axis=0, tiled=True)]
    dynamic_update_slice x16 -> x0, local copies, waits for them, and re-layouts: 11.6 us -> none  [per_block(): return lax.dynamic_update_index_in_dim(result, mixed, index, 0)]
    dot_general x1 -> x0, local copies, waits for them, and re-layouts: 11.3 us -> none  [shards(): jnp.dot(select, flat, preferred_element_type=jnp.bfloat16)]
  transfers between devices with their start and end apart: 5 -> 10, of which waited for: 5 -> 8; matrix products, arithmetic and copies ran while one was open for 2% -> 4% of each run, Pallas kernels for 0% -> 36%
where the time goes in v1:
time: 437 us; the launch traced here: 432 us
  Pallas kernels  190 us (43%)
  waiting for transfers between devices  155 us (35%)
  starting transfers between devices  59.5 us (14%)
  local copies, waits for them, and re-layouts  24.5 us (6%)
    pallas_call x4, Pallas kernels, place(): pl.pallas_call(functools.partial(place_kernel, count=count, first=first,...  135 us
    all_to_all x4, waiting for transfers between devices, shards(): lax.all_to_all(sent, 'ctx', split_axis=0, concat_axis=0, tiled=True)  101 us
    pallas_call x4, Pallas kernels, attend(): pl.pallas_call(functools.partial(attend_kernel, heads=heads, count=count)...  55.7 us
    all_to_all x5, waiting for transfers between devices, to_heads(): lax.all_to_all(parts.transpose(1, 0, 2), 'head', split_axis=0, concat_axi...  43.9 us
    all_to_all x4, starting transfers between devices, shards(): lax.all_to_all(sent, 'ctx', split_axis=0, concat_axis=0, tiled=True)  31.6 us
    all_to_all x5, starting transfers between devices, to_heads(): lax.all_to_all(parts.transpose(1, 0, 2), 'head', split_axis=0, concat_axi...  24.4 us
    unnamed x19, local copies, waits for them, and re-layouts  21.4 us
    ppermute x1, waiting for transfers between devices, shards(): lax.ppermute(kv_own[rows - HALO * BLK:], 'ctx', [(i, i + 1) for i in rang...  10.2 us
  transfers between devices with their start and end apart: 10, of which 8 were waited for; matrix products, arithmetic and copies ran while one was open for 4% of the time, Pallas kernels for 36%

profile of v1, /device:TPU:33, one launch (start us, length us, event | category | flops | bytes accessed | tf_op | source)
XLA Modules:
  0.0 432.3 jit_solution(906750226524413534)
XLA Ops:
  0.0 0.0 copy-start
  0.0 1.0 copy-done
  1.0 1.3 copy_bitcast_fusion.4
  2.3 1.1 maximum_bitcast_fusion
  3.5 5.1 %all-to-all-start.1 = ((bf16[8,256,256]{2,1,0:T(8,128)(2,1)}), bf16[8,256,256]{2,1,0:T(8,128)(2,1)S(1)}, u32[]{:S(2)}, u32[]{:S(2)}) async-start(bf16[8,256,256]{2,1,0:T(8,128)(2,1)} %maximum_bitcast_fusion), calls=%async_computation.1 | async-start | bytes 2097152 | tf_op jit(solution)/shard_map/all_to_all | solution.py:131
  8.6 6.5 %copy.27 = bf16[32,8,8,1024]{3,2,1,0:T(8,128)(2,1)S(1)} copy(bf16[32,8,8,1024]{3,1,2,0:T(8,128)(2,1)} %bitcast.39) | data formatting | bytes 8388608
  15.1 1.8 fusion.3
  16.9 1.2 copy.34
  18.2 5.5 %all-to-all-done.1 = bf16[8,256,256]{2,1,0:T(8,128)(2,1)S(1)} async-done(((bf16[8,256,256]{2,1,0:T(8,128)(2,1)}), bf16[8,256,256]{2,1,0:T(8,128)(2,1)S(1)}, u32[]{:S(2)}, u32[]{:S(2)}) %all-to-all-start.1) | async-done | bytes 1048608 | tf_op jit(solution)/shard_map/all_to_all | solution.py:131
  23.7 4.3 %all-to-all-start.7 = ((bf16[8,256,256]{2,1,0:T(8,128)(2,1)}), bf16[8,256,256]{2,1,0:T(8,128)(2,1)S(1)}, u32[]{:S(2)}, u32[]{:S(2)}) async-start(bf16[8,256,256]{2,1,0:T(8,128)(2,1)} %bitcast.42), calls=%async_computation.7 | async-start | bytes 2097152 | tf_op jit(solution)/shard_map/all_to_all | solution.py:131
  28.0 2.4 copy.35
  30.4 12.7 %all-to-all-done.7 = bf16[8,256,256]{2,1,0:T(8,128)(2,1)S(1)} async-done(((bf16[8,256,256]{2,1,0:T(8,128)(2,1)}), bf16[8,256,256]{2,1,0:T(8,128)(2,1)S(1)}, u32[]{:S(2)}, u32[]{:S(2)}) %all-to-all-start.7) | async-done | bytes 1048608 | tf_op jit(solution)/shard_map/all_to_all | solution.py:131
  43.1 5.0 %all-to-all-start.5 = ((bf16[8,256,256]{2,1,0:T(8,128)(2,1)}), bf16[8,256,256]{2,1,0:T(8,128)(2,1)}, u32[]{:S(2)}, u32[]{:S(2)}) async-start(bf16[8,256,256]{2,1,0:T(8,128)(2,1)} %bitcast.43), calls=%async_computation.5 | async-start | bytes 2097152 | tf_op jit(solution)/shard_map/all_to_all | solution.py:131
  48.1 2.4 copy.36
  50.5 12.8 %all-to-all-done.5 = bf16[8,256,256]{2,1,0:T(8,128)(2,1)} async-done(((bf16[8,256,256]{2,1,0:T(8,128)(2,1)}), bf16[8,256,256]{2,1,0:T(8,128)(2,1)}, u32[]{:S(2)}, u32[]{:S(2)}) %all-to-all-start.5) | async-done | bytes 1048608 | tf_op jit(solution)/shard_map/all_to_all | solution.py:131
  63.4 5.0 %all-to-all-start.3 = ((bf16[8,256,256]{2,1,0:T(8,128)(2,1)}), bf16[8,256,256]{2,1,0:T(8,128)(2,1)}, u32[]{:S(2)}, u32[]{:S(2)}) async-start(bf16[8,256,256]{2,1,0:T(8,128)(2,1)} %bitcast.41), calls=%async_computation.3 | async-start | bytes 2097152 | tf_op jit(solution)/shard_map/all_to_all | solution.py:131
  68.4 2.4 copy.37
  70.8 12.8 %all-to-all-done.3 = bf16[8,256,256]{2,1,0:T(8,128)(2,1)} async-done(((bf16[8,256,256]{2,1,0:T(8,128)(2,1)}), bf16[8,256,256]{2,1,0:T(8,128)(2,1)}, u32[]{:S(2)}, u32[]{:S(2)}) %all-to-all-start.3) | async-done | bytes 1048608 | tf_op jit(solution)/shard_map/all_to_all | solution.py:131
  83.6 5.0 %all-to-all-start = ((bf16[8,256,256]{2,1,0:T(8,128)(2,1)}), bf16[8,256,256]{2,1,0:T(8,128)(2,1)}, u32[]{:S(2)}, u32[]{:S(2)}) async-start(bf16[8,256,256]{2,1,0:T(8,128)(2,1)} %bitcast.40), calls=%async_computation | async-start | bytes 2097152 | tf_op jit(solution)/shard_map/all_to_all | solution.py:131
  88.6 3.5 collective-permute-start
  92.2 0.0 copy-done.6
  92.2 0.2 select_reduce_fusion.slot_ref
  92.4 10.2 %collective-permute-done.halo_ref = bf16[896,256]{1,0:T(8,128)(2,1)S(1)} collective-permute-done((bf16[896,256]{1,0:T(8,128)(2,1)S(1)}, bf16[896,256]{1,0:T(8,128)(2,1)S(1)}, u32[]{:S(2)}, u32[]{:S(2)}) %collective-permute-start) | collective-permute-done | bytes 458784 | tf_op jit(solution)/shard_map/ppermute | solution.py:138
  102.6 0.0 copy-done.5
  102.6 12.9 %attend.7 = bf16[32,128,256]{2,1,0:T(8,128)(2,1)S(1)} custom-call(s32[512]{0:T(512)S(1)} %copy-done.5, s32[16]{0:T(128)S(1)} %select_reduce_fusion.slot_ref, s32[1]{0:T(128)} %bitcast.shard_ref, bf16[2048,256]{1,0:T(8,128)(2,1)S(1)} %bitcast.37, bf16[2048,256]{1,0:T(8,128)(2,1)S(1)} %bitcast.33, bf16[896,256]{1,0:T(8,128)(2,1)S(1)} %collective-permute-done.halo_ref), custom_call_target="tpu_custom_call" | custom-call | flops 1073741824 | bytes 4194304 | tf_op jit(solution)/shard_map/attend/pallas_call | solution.py:66
  115.5 0.0 copy-start.3
  115.5 1.3 copy-done.3
  116.8 0.0 all-to-all-done
  116.8 12.3 %all-to-all-start.8 = ((bf16[32,128,256]{2,1,0:T(8,128)(2,1)}), bf16[32,128,256]{2,1,0:T(8,128)(2,1)}, u32[]{:S(2)}, u32[]{:S(2)}) async-start(bf16[32,128,256]{2,1,0:T(8,128)(2,1)} %copy-done.3), calls=%async_computation.8 | async-start | bytes 4194304 | tf_op jit(solution)/shard_map/all_to_all | solution.py:156
  129.1 14.3 %attend.6 = bf16[32,128,256]{2,1,0:T(8,128)(2,1)S(1)} custom-call(s32[512]{0:T(512)S(1)} %copy-done.5, s32[16]{0:T(128)S(1)} %select_reduce_fusion.slot_ref, s32[1]{0:T(128)} %bitcast.shard_ref, bf16[2048,256]{1,0:T(8,128)(2,1)} %bitcast.8.q_ref, bf16[2048,256]{1,0:T(8,128)(2,1)S(1)} %bitcast.34, bf16[896,256]{1,0:T(8,128)(2,1)S(1)} %collective-permute-done.halo_ref), custom_call_target="tpu_custom_call" | custom-call | flops 1073741824 | bytes 4194304 | tf_op jit(solution)/shard_map/attend/pallas_call | solution.py:66
  143.4 1.3 copy-done.4
  144.8 33.9 %all-to-all-done.8.refs_0_ = bf16[32,128,256]{2,1,0:T(8,128)(2,1)} async-done(((bf16[32,128,256]{2,1,0:T(8,128)(2,1)}), bf16[32,128,256]{2,1,0:T(8,128)(2,1)}, u32[]{:S(2)}, u32[]{:S(2)}) %all-to-all-start.8) | async-done | bytes 2097184 | tf_op jit(solution)/shard_map/all_to_all | solution.py:156
  178.7 6.4 %all-to-all-start.6 = ((bf16[32,128,256]{2,1,0:T(8,128)(2,1)}), bf16[32,128,256]{2,1,0:T(8,128)(2,1)}, u32[]{:S(2)}, u32[]{:S(2)}) async-start(bf16[32,128,256]{2,1,0:T(8,128)(2,1)} %copy-done.4), calls=%async_computation.6 | async-start | bytes 4194304 | tf_op jit(solution)/shard_map/all_to_all | solution.py:156
  185.1 14.3 %attend.5 = bf16[32,128,256]{2,1,0:T(8,128)(2,1)S(1)} custom-call(s32[512]{0:T(512)S(1)} %copy-done.5, s32[16]{0:T(128)S(1)} %select_reduce_fusion.slot_ref, s32[1]{0:T(128)} %bitcast.shard_ref, bf16[2048,256]{1,0:T(8,128)(2,1)} %bitcast.6.q_ref, bf16[2048,256]{1,0:T(8,128)(2,1)S(1)} %bitcast.35, bf16[896,256]{1,0:T(8,128)(2,1)S(1)} %collective-permute-done.halo_ref), custom_call_target="tpu_custom_call" | custom-call | flops 1073741824 | bytes 4194304 | tf_op jit(solution)/shard_map/attend/pallas_call | solution.py:66
  199.4 0.0 copy-start.2
  199.4 1.3 copy-done.2
  200.7 33.8 %all-to-all-done.6.refs_0_ = bf16[32,128,256]{2,1,0:T(8,128)(2,1)} async-done(((bf16[32,128,256]{2,1,0:T(8,128)(2,1)}), bf16[32,128,256]{2,1,0:T(8,128)(2,1)}, u32[]{:S(2)}, u32[]{:S(2)}) %all-to-all-start.6) | async-done | bytes 2097184 | tf_op jit(solution)/shard_map/all_to_all | solution.py:156
  234.5 6.4 %all-to-all-start.4 = ((bf16[32,128,256]{2,1,0:T(8,128)(2,1)}), bf16[32,128,256]{2,1,0:T(8,128)(2,1)}, u32[]{:S(2)}, u32[]{:S(2)}) async-start(bf16[32,128,256]{2,1,0:T(8,128)(2,1)} %copy-done.2), calls=%async_computation.4 | async-start | bytes 4194304 | tf_op jit(solution)/shard_map/all_to_all | solution.py:156
  240.9 14.3 %attend.4 = bf16[32,128,256]{2,1,0:T(8,128)(2,1)S(1)} custom-call(s32[512]{0:T(512)S(1)} %copy-done.5, s32[16]{0:T(128)S(1)} %select_reduce_fusion.slot_ref, s32[1]{0:T(128)} %bitcast.shard_ref, bf16[2048,256]{1,0:T(8,128)(2,1)} %bitcast.2.q_ref, bf16[2048,256]{1,0:T(8,128)(2,1)S(1)} %bitcast.36, bf16[896,256]{1,0:T(8,128)(2,1)S(1)} %collective-permute-done.halo_ref), custom_call_target="tpu_custom_call" | custom-call | flops 1073741824 | bytes 4194304 | tf_op jit(solution)/shard_map/attend/pallas_call | solution.py:66
  255.2 1.4 copy-done.1
  256.6 33.7 %all-to-all-done.4.refs_0_ = bf16[32,128,256]{2,1,0:T(8,128)(2,1)} async-done(((bf16[32,128,256]{2,1,0:T(8,128)(2,1)}), bf16[32,128,256]{2,1,0:T(8,128)(2,1)}, u32[]{:S(2)}, u32[]{:S(2)}) %all-to-all-start.4) | async-done | bytes 2097184 | tf_op jit(solution)/shard_map/all_to_all | solution.py:156
  290.3 6.5 %all-to-all-start.2 = ((bf16[32,128,256]{2,1,0:T(8,128)(2,1)}), bf16[32,128,256]{2,1,0:T(8,128)(2,1)}, u32[]{:S(2)}, u32[]{:S(2)}) async-start(bf16[32,128,256]{2,1,0:T(8,128)(2,1)} %copy-done.1), calls=%async_computation.2 | async-start | bytes 4194304 | tf_op jit(solution)/shard_map/all_to_all | solution.py:156
  296.7 0.7 and_select_fusion.source_ref
  297.4 33.7 %place.4.refs_1_ = bf16[2048,1024]{1,0:T(8,128)(2,1)} custom-call(s32[16]{0:T(128)} %and_select_fusion.source_ref, bf16[32,128,256]{2,1,0:T(8,128)(2,1)} %all-to-all-done.8.refs_0_), custom_call_target="tpu_custom_call" | custom-call | bytes 2097152 | tf_op jit(solution)/shard_map/place/pallas_call | solution.py:109
  331.1 33.7 %place.5.refs_1_ = bf16[2048,1024]{1,0:T(8,128)(2,1)} custom-call(s32[16]{0:T(128)} %and_select_fusion.source_ref, bf16[32,128,256]{2,1,0:T(8,128)(2,1)} %all-to-all-done.6.refs_0_, bf16[2048,1024]{1,0:T(8,128)(2,1)} %place.4.refs_1_), custom_call_target="tpu_custom_call", output_to_operand_aliasing={{}: (2, {})} | custom-call | bytes 2097152 | tf_op jit(solution)/shard_map/place/pallas_call | solution.py:109
  364.8 33.7 %place.6.refs_1_ = bf16[2048,1024]{1,0:T(8,128)(2,1)} custom-call(s32[16]{0:T(128)} %and_select_fusion.source_ref, bf16[32,128,256]{2,1,0:T(8,128)(2,1)} %all-to-all-done.4.refs_0_, bf16[2048,1024]{1,0:T(8,128)(2,1)} %place.5.refs_1_), custom_call_target="tpu_custom_call", output_to_operand_aliasing={{}: (2, {})} | custom-call | bytes 2097152 | tf_op jit(solution)/shard_map/place/pallas_call | solution.py:109
  398.4 0.0 all-to-all-done.2.refs_0_
  398.5 33.7 %place.7 = bf16[2048,1024]{1,0:T(8,128)(2,1)} custom-call(s32[16]{0:T(128)} %and_select_fusion.source_ref, bf16[32,128,256]{2,1,0:T(8,128)(2,1)} %all-to-all-done.2.refs_0_, bf16[2048,1024]{1,0:T(8,128)(2,1)} %place.6.refs_1_), custom_call_target="tpu_custom_call", output_to_operand_aliasing={{}: (2, {})} | custom-call | bytes 2097152 | tf_op jit(solution)/shard_map/place/pallas_call | solution.py:109
  (7 shorter events, 0.0 us)
Async XLA Ops:
  0.0 1.0 copy-start
  3.5 20.2 %all-to-all-start.1 = ((bf16[8,256,256]{2,1,0:T(8,128)(2,1)}), bf16[8,256,256]{2,1,0:T(8,128)(2,1)S(1)}, u32[]{:S(2)}, u32[]{:S(2)}) async-start(bf16[8,256,256]{2,1,0:T(8,128)(2,1)} %maximum_bitcast_fusion), calls=%async_computation.1 | async-start | bytes 2097152 | tf_op jit(solution)/shard_map/all_to_all | solution.py:131
  23.7 19.4 %all-to-all-start.7 = ((bf16[8,256,256]{2,1,0:T(8,128)(2,1)}), bf16[8,256,256]{2,1,0:T(8,128)(2,1)S(1)}, u32[]{:S(2)}, u32[]{:S(2)}) async-start(bf16[8,256,256]{2,1,0:T(8,128)(2,1)} %bitcast.42), calls=%async_computation.7 | async-start | bytes 2097152 | tf_op jit(solution)/shard_map/all_to_all | solution.py:131
  43.1 20.2 %all-to-all-start.5 = ((bf16[8,256,256]{2,1,0:T(8,128)(2,1)}), bf16[8,256,256]{2,1,0:T(8,128)(2,1)}, u32[]{:S(2)}, u32[]{:S(2)}) async-start(bf16[8,256,256]{2,1,0:T(8,128)(2,1)} %bitcast.43), calls=%async_computation.5 | async-start | bytes 2097152 | tf_op jit(solution)/shard_map/all_to_all | solution.py:131
  63.4 20.2 %all-to-all-start.3 = ((bf16[8,256,256]{2,1,0:T(8,128)(2,1)}), bf16[8,256,256]{2,1,0:T(8,128)(2,1)}, u32[]{:S(2)}, u32[]{:S(2)}) async-start(bf16[8,256,256]{2,1,0:T(8,128)(2,1)} %bitcast.41), calls=%async_computation.3 | async-start | bytes 2097152 | tf_op jit(solution)/shard_map/all_to_all | solution.py:131
  68.4 23.8 %copy-start.6 = (s32[512]{0:T(512)S(1)}, s32[512]{0:T(512)}, u32[]{:S(2)}) copy-start(s32[512]{0:T(512)} %param.9) | copy-start | bytes 6148
  68.4 34.2 %copy-start.5 = (s32[512]{0:T(512)S(1)}, s32[512]{0:T(512)}, u32[]{:S(2)}) copy-start(s32[512]{0:T(512)} %doc_ref.7) | copy-start | bytes 6148
  83.6 33.2 %all-to-all-start = ((bf16[8,256,256]{2,1,0:T(8,128)(2,1)}), bf16[8,256,256]{2,1,0:T(8,128)(2,1)}, u32[]{:S(2)}, u32[]{:S(2)}) async-start(bf16[8,256,256]{2,1,0:T(8,128)(2,1)} %bitcast.40), calls=%async_computation | async-start | bytes 2097152 | tf_op jit(solution)/shard_map/all_to_all | solution.py:131
  88.6 14.0 %collective-permute-start = (bf16[896,256]{1,0:T(8,128)(2,1)S(1)}, bf16[896,256]{1,0:T(8,128)(2,1)S(1)}, u32[]{:S(2)}, u32[]{:S(2)}) collective-permute-start(bf16[896,256]{1,0:T(8,128)(2,1)S(1)} %slice.21), channel_id=1, source_target_pairs={{0,8},{8,16},{16,24},{24,32},{32,40},{40,48},{48,56},{56,64},{64,7... | collective-permute-start | bytes 1376264 | tf_op jit(solution)/shard_map/ppermute | solution.py:138
  115.5 1.3 copy-start.3
  116.8 61.9 %all-to-all-start.8 = ((bf16[32,128,256]{2,1,0:T(8,128)(2,1)}), bf16[32,128,256]{2,1,0:T(8,128)(2,1)}, u32[]{:S(2)}, u32[]{:S(2)}) async-start(bf16[32,128,256]{2,1,0:T(8,128)(2,1)} %copy-done.3), calls=%async_computation.8 | async-start | bytes 4194304 | tf_op jit(solution)/shard_map/all_to_all | solution.py:156
  143.4 1.3 copy-start.4
  178.7 55.8 %all-to-all-start.6 = ((bf16[32,128,256]{2,1,0:T(8,128)(2,1)}), bf16[32,128,256]{2,1,0:T(8,128)(2,1)}, u32[]{:S(2)}, u32[]{:S(2)}) async-start(bf16[32,128,256]{2,1,0:T(8,128)(2,1)} %copy-done.4), calls=%async_computation.6 | async-start | bytes 4194304 | tf_op jit(solution)/shard_map/all_to_all | solution.py:156
  199.4 1.3 copy-start.2
  234.5 55.8 %all-to-all-start.4 = ((bf16[32,128,256]{2,1,0:T(8,128)(2,1)}), bf16[32,128,256]{2,1,0:T(8,128)(2,1)}, u32[]{:S(2)}, u32[]{:S(2)}) async-start(bf16[32,128,256]{2,1,0:T(8,128)(2,1)} %copy-done.2), calls=%async_computation.4 | async-start | bytes 4194304 | tf_op jit(solution)/shard_map/all_to_all | solution.py:156
  255.2 1.4 copy-start.1
  290.3 108.2 %all-to-all-start.2 = ((bf16[32,128,256]{2,1,0:T(8,128)(2,1)}), bf16[32,128,256]{2,1,0:T(8,128)(2,1)}, u32[]{:S(2)}, u32[]{:S(2)}) async-start(bf16[32,128,256]{2,1,0:T(8,128)(2,1)} %copy-done.1), calls=%async_computation.2 | async-start | bytes 4194304 | tf_op jit(solution)/shard_map/all_to_all | solution.py:156

commit v2 on v1

--- a/solution.py
+++ b/solution.py
@@ -12,11 +12,13 @@
 BLK = 128
 MAXDOC = 8
 HALO = MAXDOC - 1
-CHUNKS = (2, 2, 2, 2)
+CHUNKS = (1, 2, 5)
 EXP2_SCALE = math.log2(math.e) / math.sqrt(HD)
 
 
-def attend_kernel(doc_ref, slot_ref, shard_ref, q_ref, own_ref, halo_ref, out_ref, win_ref, *, heads, count):
+def attend_kernel(
+    doc_ref, slot_ref, origin_ref, shard_ref, q_ref, own_ref, halo_ref, out_ref, win_ref, *, heads, count
+):
     index = pl.program_id(0)
 
     @pl.when(index == 0)
@@ -59,21 +61,21 @@
         pl.when(tiles == n)(functools.partial(with_tiles, n))
 
 
-def attend(queries, kv_own, kv_halo, doc_ids, slot, shard, slots):
+def attend(queries, kv_own, kv_halo, doc_ids, slot, origin, shard, slots):
     rows, width = queries.shape
     count = rows // BLK
     heads = width // HD
     return pl.pallas_call(
         functools.partial(attend_kernel, heads=heads, count=count),
         grid_spec=pltpu.PrefetchScalarGridSpec(
-            num_scalar_prefetch=3,
+            num_scalar_prefetch=4,
             grid=(count,),
             in_specs=[
-                pl.BlockSpec((BLK, width), lambda i, doc, slot, shard: (i, 0)),
-                pl.BlockSpec(kv_own.shape, lambda i, doc, slot, shard: (0, 0)),
-                pl.BlockSpec(kv_halo.shape, lambda i, doc, slot, shard: (0, 0)),
+                pl.BlockSpec((BLK, width), lambda i, doc, slot, origin, shard: (origin[i], 0)),
+                pl.BlockSpec(kv_own.shape, lambda i, doc, slot, origin, shard: (0, 0)),
+                pl.BlockSpec(kv_halo.shape, lambda i, doc, slot, origin, shard: (0, 0)),
             ],
-            out_specs=pl.BlockSpec((1, BLK, width), lambda i, doc, slot, shard: (slot[i], 0, 0)),
+            out_specs=pl.BlockSpec((1, BLK, width), lambda i, doc, slot, origin, shard: (slot[i], 0, 0)),
             scratch_shapes=[pltpu.VMEM((kv_own.shape[0] + kv_halo.shape[0], 2 * HD), jnp.bfloat16)],
         ),
         out_shape=jax.ShapeDtypeStruct((slots, BLK, width), jnp.bfloat16),
@@ -84,23 +86,27 @@
             transcendentals=rows * heads * BLK * 4,
         ),
         name="attend",
-    )(doc_ids, slot, shard, queries, kv_own, kv_halo)
+    )(doc_ids, slot, origin, shard, queries, kv_own, kv_halo)
 
 
 def place_kernel(source_ref, *refs, count, first, width):
-    received_ref, out_ref, sems = refs[0], refs[-2], refs[-1]
-
-    def copy(i):
+    received_ref, out_ref, held_ref, in_sems, out_sems = refs[0], refs[-4], refs[-3], refs[-2], refs[-1]
+
+    def fetch(i):
+        return pltpu.make_async_copy(received_ref.at[source_ref[i]], held_ref.at[i], in_sems.at[i])
+
+    def store(i):
         return pltpu.make_async_copy(
-            received_ref.at[source_ref[i]],
-            out_ref.at[pl.ds(i * BLK, BLK), pl.ds(first, width)],
-            sems.at[i],
+            held_ref.at[i], out_ref.at[pl.ds(i * BLK, BLK), pl.ds(first, width)], out_sems.at[i]
         )
 
     for i in range(count):
-        copy(i).start()
+        fetch(i).start()
     for i in range(count):
-        copy(i).wait()
+        fetch(i).wait()
+        store(i).start()
+    for i in range(count):
+        store(i).wait()
 
 
 def place(received, source, result, first, count, full_width):
@@ -111,8 +117,13 @@
         in_specs=[pl.BlockSpec(memory_space=pltpu.SMEM)] + [pl.BlockSpec(memory_space=pl.ANY)] * len(given),
         out_specs=pl.BlockSpec(memory_space=pl.ANY),
         out_shape=jax.ShapeDtypeStruct((count * BLK, full_width), jnp.bfloat16),
-        scratch_shapes=[pltpu.SemaphoreType.DMA((count,))],
+        scratch_shapes=[
+            pltpu.VMEM((count, BLK, width), jnp.bfloat16),
+            pltpu.SemaphoreType.DMA((count,)),
+            pltpu.SemaphoreType.DMA((count,)),
+        ],
         input_output_aliases={} if result is None else {2: 0},
+        compiler_params=pltpu.CompilerParams(vmem_limit_bytes=32 * 1024 * 1024),
         cost_estimate=pl.CostEstimate(flops=0, bytes_accessed=4 * count * BLK * width, transcendentals=0),
         name="place",
     )(source, *given)
@@ -124,35 +135,71 @@
     local_rows = query.shape[0]
     rows = head_count * local_rows
     count = rows // BLK
+    per_device = local_rows // BLK
     q_width = query.shape[1] // head_count
+    kv_width = key.shape[1] // head_count
     shard = lax.axis_index("ctx").astype(jnp.int32)
-
-    def to_heads(parts):
-        moved = lax.all_to_all(parts.transpose(1, 0, 2), "head", split_axis=0, concat_axis=0, tiled=True)
+    member = lax.axis_index("head").astype(jnp.int32)
+    core, chip, chips = member % 2, member // 2, head_count // 2
+
+    def by_head(array, width, first, size):
+        return jnp.stack([array[:, h * width + first : h * width + first + size] for h in range(head_count)])
+
+    def exchange(parts):
+        moved = lax.all_to_all(parts, "head", split_axis=0, concat_axis=0, tiled=True)
         return moved.reshape(rows, parts.shape[2])
 
-    kv_parts = jnp.concatenate(
-        [key.reshape(local_rows, head_count, HD), value.reshape(local_rows, head_count, HD)], axis=2
-    )
-    kv_own = to_heads(kv_parts)
+    def core_swap(parts):
+        pairs = parts.reshape(chips, 2, local_rows, parts.shape[2])
+        kept = lax.dynamic_index_in_dim(pairs, core, 1, False)
+        given = lax.dynamic_index_in_dim(pairs, 1 - core, 1, False)
+        got = lax.ppermute(given, "head", [(h, h ^ 1) for h in range(head_count)])
+        return jnp.stack([kept, got], axis=1)
+
+    def chip_exchange(both):
+        arrived = []
+        for step in range(chips):
+            piece = lax.dynamic_index_in_dim(both, (chip + step) % chips, 0, False)
+            if step:
+                piece = lax.ppermute(
+                    piece, "head", [(h, (h + 2 * step) % head_count) for h in range(head_count)]
+                )
+            arrived.append(piece)
+        return jnp.stack(arrived).reshape(rows, both.shape[3])
+
+    kv_own = exchange(
+        jnp.concatenate([by_head(key, kv_width, 0, kv_width), by_head(value, kv_width, 0, kv_width)], axis=2)
+    )
     kv_halo = lax.ppermute(
         kv_own[rows - HALO * BLK :], "ctx", [(i, i + 1) for i in range(shard_count - 1)]
     )
 
-    own_ids = shard * count + jnp.arange(count, dtype=jnp.int32)
+    index = jnp.arange(count, dtype=jnp.int32)
+    own_ids = shard * count + index
     position = jnp.arange(plan.shape[0], dtype=jnp.int32)
     target = jnp.sum(
         jnp.where(plan[None, :] == own_ids[:, None], position[None, :] // count, 0), axis=1, dtype=jnp.int32
     )
     source = lax.dynamic_slice_in_dim(plan, shard * count, count) // count
-
-    q_parts = query.reshape(local_rows, head_count, q_width)
+    giver = index // per_device
+    steps_back = (chip - giver // 2 + chips) % chips
+    arrival = (steps_back * 2 + jnp.where(giver % 2 == core, 0, 1)) * per_device + index % per_device
+
     result = None
     first = 0
-    for heads in CHUNKS:
+    earlier = kv_own
+    for turn, heads in enumerate(CHUNKS):
         width = heads * HD
-        queries = to_heads(q_parts[:, :, first : first + width])
-        sent = attend(queries, kv_own, kv_halo, doc_ids, target, shard.reshape(1), shard_count)
+        parts = by_head(query, q_width, first, width)
+        if turn == 0:
+            queries = exchange(parts)
+            origin = index
+        else:
+            both, earlier = lax.optimization_barrier((core_swap(parts), earlier))
+            queries = chip_exchange(both)
+            origin = arrival
+        sent = attend(queries, kv_own, kv_halo, doc_ids, target, origin, shard.reshape(1), shard_count)
+        earlier = queries if turn == 0 else earlier
         received = lax.all_to_all(sent, "ctx", split_axis=0, concat_axis=0, tiled=True)
         result = place(received, source, result, first, count, q_width)
         first += width

time: 437 us -> 342 us (0.78)
  Pallas kernels: 190 us -> 58.4 us
  local copies, waits for them, and re-layouts: 24.5 us -> 59.3 us
    pallas_call x4 -> x3, Pallas kernels: 135 us -> 8.84 us  [place(): pl.pallas_call(functools.partial(place_kernel, count=count, first=first,...]
    all_to_all x5 -> x2, waiting for transfers between devices: 43.9 us -> 2.74 us  [exchange(): lax.all_to_all(parts, 'head', split_axis=0, concat_axis=0, tiled=True)]
    ppermute x0 -> x8, waiting for transfers between devices: none -> 38.9 us  [the longest x6 36.3 us: chip_exchange(): lax.ppermute(piece, 'head', [(h, (h + 2 * step) % head_count) for h in ra...]
    unnamed x19 -> x49, local copies, waits for them, and re-layouts: 21.4 us -> 49.2 us
    all_to_all x5 -> x2, starting transfers between devices: 24.4 us -> 9.95 us  [exchange(): lax.all_to_all(parts, 'head', split_axis=0, concat_axis=0, tiled=True)]
    ppermute x0 -> x8, starting transfers between devices: none -> 12.5 us  [the longest x6 9.59 us: chip_exchange(): lax.ppermute(piece, 'head', [(h, (h + 2 * step) % head_count) for h in ra...]
    all_to_all x4 -> x3, waiting for transfers between devices: 101 us -> 113 us  [shards(): lax.all_to_all(sent, 'ctx', split_axis=0, concat_axis=0, tiled=True)]
    pallas_call x4 -> x3, Pallas kernels: 55.7 us -> 49.5 us  [attend(): pl.pallas_call(functools.partial(attend_kernel, heads=heads, count=count)...]
  transfers between devices with their start and end apart: 10 -> 14, of which waited for: 8 -> 8; matrix products, arithmetic and copies ran while one was open for 4% -> 13% of each run, Pallas kernels for 36% -> 13%
where the time goes in v2:
time: 342 us; the launch traced here: 338 us
  waiting for transfers between devices  159 us (46%)
  local copies, waits for them, and re-layouts  59.3 us (17%)
  Pallas kernels  58.4 us (17%)
  starting transfers between devices  57.4 us (17%)
    all_to_all x3, waiting for transfers between devices, shards(): lax.all_to_all(sent, 'ctx', split_axis=0, concat_axis=0, tiled=True)  113 us
    pallas_call x3, Pallas kernels, attend(): pl.pallas_call(functools.partial(attend_kernel, heads=heads, count=count)...  49.5 us
    unnamed x49, local copies, waits for them, and re-layouts  49.2 us
    ppermute x6, waiting for transfers between devices, chip_exchange(): lax.ppermute(piece, 'head', [(h, (h + 2 * step) % head_count) for h in ra...  36.3 us
    all_to_all x3, starting transfers between devices, shards(): lax.all_to_all(sent, 'ctx', split_axis=0, concat_axis=0, tiled=True)  31.4 us
    all_to_all x2, starting transfers between devices, exchange(): lax.all_to_all(parts, 'head', split_axis=0, concat_axis=0, tiled=True)  9.95 us
    ppermute x6, starting transfers between devices, chip_exchange(): lax.ppermute(piece, 'head', [(h, (h + 2 * step) % head_count) for h in ra...  9.59 us
    pallas_call x3, Pallas kernels, place(): pl.pallas_call(functools.partial(place_kernel, count=count, first=first,...  8.84 us
  transfers between devices with their start and end apart: 14, of which 8 were waited for; matrix products, arithmetic and copies ran while one was open for 13% of the time, Pallas kernels for 13%

profile of v2, /device:TPU:33, one launch (start us, length us, event | category | flops | bytes accessed | tf_op | source)
XLA Modules:
  0.0 337.8 jit_solution(4917477578341511417)
XLA Ops:
  14.0 5.1 %all-to-all-start = ((bf16[8,256,256]{2,1,0:T(8,128)(2,1)}), bf16[8,256,256]{2,1,0:T(8,128)(2,1)S(1)}, u32[]{:S(2)}, u32[]{:S(2)}) async-start(bf16[8,256,256]{2,1,0:T(8,128)(2,1)} %pad_maximum_fusion.2), calls=%async_computation | async-start | bytes 2097152 | tf_op jit(solution)/shard_map/all_to_all | solution.py:149
  19.1 1.5 constant_dynamic-update-slice_fusion.23
  20.6 1.5 constant_dynamic-update-slice_fusion.22
  22.1 1.5 constant_dynamic-update-slice_fusion.21
  26.5 1.5 constant_dynamic-update-slice_fusion.18
  27.9 1.5 constant_dynamic-update-slice_fusion.17
  29.6 1.5 constant_dynamic-update-slice_fusion.16
  31.1 1.6 bitcast_dynamic-update-slice_fusion.15
  32.6 1.6 bitcast_dynamic-update-slice_fusion.14
  34.2 1.6 bitcast_dynamic-update-slice_fusion.13
  35.8 4.8 %all-to-all-start.2 = ((bf16[8,256,128]{2,1,0:T(8,128)(2,1)}), bf16[8,256,128]{2,1,0:T(8,128)(2,1)S(1)}, u32[]{:S(2)}, u32[]{:S(2)}) async-start(bf16[8,256,128]{2,1,0:T(8,128)(2,1)} %constant_dynamic-update-slice_fusion.16), calls=%async_computation.2 | async-start | bytes 1048576 | tf_op jit(solution)/shard_map/all_to_all | solution.py:149
  40.6 3.5 %collective-permute-start.4 = (bf16[896,256]{1,0:T(8,128)(2,1)S(1)}, bf16[896,256]{1,0:T(8,128)(2,1)S(1)}, u32[]{:S(2)}, u32[]{:S(2)}) collective-permute-start(bf16[896,256]{1,0:T(8,128)(2,1)S(1)} %slice.164), channel_id=1, source_target_pairs={{0,8},{8,16},{16,24},{24,32},{32,40},{40,48},{48,56},{56,64},{64,7... | collective-permute-start | bytes 1376264 | tf_op jit(solution)/shard_map/ppermute | solution.py:173
  44.1 1.6 bitcast_dynamic-update-slice_fusion.12
  45.7 1.6 bitcast_dynamic-update-slice_fusion.11
  47.3 2.7 all-to-all-done.2
  50.0 4.6 %collective-permute-done.4.halo_ref = bf16[896,256]{1,0:T(8,128)(2,1)S(1)} collective-permute-done((bf16[896,256]{1,0:T(8,128)(2,1)S(1)}, bf16[896,256]{1,0:T(8,128)(2,1)S(1)}, u32[]{:S(2)}, u32[]{:S(2)}) %collective-permute-start.4) | collective-permute-done | bytes 458784 | tf_op jit(solution)/shard_map/ppermute | solution.py:173
  54.6 9.9 %attend.5 = bf16[32,128,128]{2,1,0:T(8,128)(2,1)} custom-call(s32[512]{0:T(512)S(1)} %copy-done.5, s32[16]{0:T(128)S(1)} %select_reduce_fusion.slot_ref, s32[16]{0:T(128)S(1)} %iota.21.origin_ref, s32[1]{0:T(128)} %bitcast.shard_ref, bf16[2048,128]{1,0:T(8,128)(2,1)S(1)} %bitcast.117, bf16[2048,256]{1,0:T(8,128)(2,1)S(1)} %bitcast.112, ...), custom_call_target="tpu_custom_call" | custom-call | flops 536870912 | bytes 3145728 | tf_op jit(solution)/shard_map/attend/pallas_call | solution.py:68
  64.6 11.9 %all-to-all-start.4 = ((bf16[32,128,128]{2,1,0:T(8,128)(2,1)}), bf16[32,128,128]{2,1,0:T(8,128)(2,1)S(1)}, u32[]{:S(2)}, u32[]{:S(2)}) async-start(bf16[32,128,128]{2,1,0:T(8,128)(2,1)} %attend.5), calls=%async_computation.4 | async-start | bytes 2097152 | tf_op jit(solution)/shard_map/all_to_all | solution.py:203
  76.5 1.6 bitcast_dynamic-update-slice_fusion.10
  78.1 1.6 bitcast_dynamic-update-slice_fusion.9
  79.6 1.6 bitcast_dynamic-update-slice_fusion.8
  81.2 2.1 constant_dynamic-slice_fusion.1
  84.6 1.7 bitcast_dynamic-update-slice_fusion.7
  86.3 1.7 bitcast_dynamic-update-slice_fusion.6
  90.7 2.4 collective-permute-start.7
  94.3 1.7 bitcast_dynamic-update-slice_fusion.5
  96.1 2.4 collective-permute-done.6
  98.5 6.7 %collective-permute-done.7 = bf16[2,256,256]{2,1,0:T(8,128)(2,1)S(1)} collective-permute-done((bf16[2,256,256]{2,1,0:T(8,128)(2,1)S(1)}, bf16[2,256,256]{2,1,0:T(8,128)(2,1)S(1)}, u32[]{:S(2)}, u32[]{:S(2)}) %collective-permute-start.7) | collective-permute-done | bytes 262176 | tf_op jit(solution)/shard_map/ppermute | solution.py:164
  105.4 14.1 %attend.4 = bf16[32,128,256]{2,1,0:T(8,128)(2,1)} custom-call(s32[512]{0:T(512)S(1)} %copy-done.5, s32[16]{0:T(128)S(1)} %select_reduce_fusion.slot_ref, s32[16]{0:T(128)S(1)} %fusion.3.origin_ref, s32[1]{0:T(128)} %bitcast.shard_ref, bf16[2048,256]{1,0:T(8,128)(2,1)S(1)} %bitcast.115, bf16[2048,256]{1,0:T(8,128)(2,1)S(1)} %bitcast.113, ...), custom_call_target="tpu_custom_call" | custom-call | flops 1073741824 | bytes 4194304 | tf_op jit(solution)/shard_map/attend/pallas_call | solution.py:68
  120.4 9.5 %all-to-all-start.3 = ((bf16[32,128,256]{2,1,0:T(8,128)(2,1)}), bf16[32,128,256]{2,1,0:T(8,128)(2,1)S(1)}, u32[]{:S(2)}, u32[]{:S(2)}) async-start(bf16[32,128,256]{2,1,0:T(8,128)(2,1)} %attend.4), calls=%async_computation.3 | async-start | bytes 4194304 | tf_op jit(solution)/shard_map/all_to_all | solution.py:203
  129.9 1.7 bitcast_dynamic-update-slice_fusion.4
  131.6 1.7 bitcast_dynamic-update-slice_fusion.3
  133.4 1.7 bitcast_dynamic-update-slice_fusion.2
  135.1 1.7 bitcast_dynamic-update-slice_fusion.1
  136.8 1.7 bitcast_dynamic-update-slice_fusion
  138.5 2.0 constant_dynamic-slice_fusion.3
  140.5 1.6 collective-permute-start
  142.1 2.7 collective-permute-done
  146.4 2.1 collective-permute-start.2
  149.9 12.7 %collective-permute-done.1 = bf16[2,256,640]{2,1,0:T(8,128)(2,1)S(1)} collective-permute-done((bf16[2,256,640]{2,1,0:T(8,128)(2,1)S(1)}, bf16[2,256,640]{2,1,0:T(8,128)(2,1)S(1)}, u32[]{:S(2)}, u32[]{:S(2)}) %collective-permute-start.1) | collective-permute-done | bytes 655392 | tf_op jit(solution)/shard_map/ppermute | solution.py:164
  162.5 14.4 %collective-permute-done.2 = bf16[2,256,640]{2,1,0:T(8,128)(2,1)S(1)} collective-permute-done((bf16[2,256,640]{2,1,0:T(8,128)(2,1)S(1)}, bf16[2,256,640]{2,1,0:T(8,128)(2,1)S(1)}, u32[]{:S(2)}, u32[]{:S(2)}) %collective-permute-start.2) | collective-permute-done | bytes 655392 | tf_op jit(solution)/shard_map/ppermute | solution.py:164
  178.0 25.5 %attend.3 = bf16[32,128,640]{2,1,0:T(8,128)(2,1)S(1)} custom-call(s32[512]{0:T(512)S(1)} %copy-done.5, s32[16]{0:T(128)S(1)} %select_reduce_fusion.slot_ref, s32[16]{0:T(128)S(1)} %fusion.3.origin_ref, s32[1]{0:T(128)} %bitcast.shard_ref, bf16[2048,640]{1,0:T(8,128)(2,1)S(1)} %bitcast.116, bf16[2048,256]{1,0:T(8,128)(2,1)S(1)} %bitcast.114, ...), custom_call_target="tpu_custom_call" | custom-call | flops 2684354560 | bytes 7340032 | tf_op jit(solution)/shard_map/attend/pallas_call | solution.py:68
  203.5 2.3 copy-done
  205.9 10.0 %all-to-all-start.1 = ((bf16[32,128,640]{2,1,0:T(8,128)(2,1)}), bf16[32,128,640]{2,1,0:T(8,128)(2,1)}, u32[]{:S(2)}, u32[]{:S(2)}) async-start(bf16[32,128,640]{2,1,0:T(8,128)(2,1)} %copy-done), calls=%async_computation.1 | async-start | bytes 10485760 | tf_op jit(solution)/shard_map/all_to_all | solution.py:203
  216.0 2.3 place.3.refs_1_
  218.3 3.2 place.4.refs_1_
  221.5 112.8 %all-to-all-done.1.refs_0_ = bf16[32,128,640]{2,1,0:T(8,128)(2,1)} async-done(((bf16[32,128,640]{2,1,0:T(8,128)(2,1)}), bf16[32,128,640]{2,1,0:T(8,128)(2,1)}, u32[]{:S(2)}, u32[]{:S(2)}) %all-to-all-start.1) | async-done | bytes 5242912 | tf_op jit(solution)/shard_map/all_to_all | solution.py:203
  334.3 3.3 place.5
  (55 shorter events, 27.5 us)
Async XLA Ops:
  12.8 16.6 %copy-start.6 = (s32[512]{0:T(512)S(1)}, s32[512]{0:T(512)}, u32[]{:S(2)}) copy-start(s32[512]{0:T(512)} %param.9) | copy-start | bytes 6148
  14.0 21.8 %all-to-all-start = ((bf16[8,256,256]{2,1,0:T(8,128)(2,1)}), bf16[8,256,256]{2,1,0:T(8,128)(2,1)S(1)}, u32[]{:S(2)}, u32[]{:S(2)}) async-start(bf16[8,256,256]{2,1,0:T(8,128)(2,1)} %pad_maximum_fusion.2), calls=%async_computation | async-start | bytes 2097152 | tf_op jit(solution)/shard_map/all_to_all | solution.py:149
  19.1 35.5 %copy-start.5 = (s32[512]{0:T(512)S(1)}, s32[512]{0:T(512)}, u32[]{:S(2)}) copy-start(s32[512]{0:T(512)} %doc_ref.5) | copy-start | bytes 6148
  35.8 14.3 %all-to-all-start.2 = ((bf16[8,256,128]{2,1,0:T(8,128)(2,1)}), bf16[8,256,128]{2,1,0:T(8,128)(2,1)S(1)}, u32[]{:S(2)}, u32[]{:S(2)}) async-start(bf16[8,256,128]{2,1,0:T(8,128)(2,1)} %constant_dynamic-update-slice_fusion.16), calls=%async_computation.2 | async-start | bytes 1048576 | tf_op jit(solution)/shard_map/all_to_all | solution.py:149
  40.6 14.0 %collective-permute-start.4 = (bf16[896,256]{1,0:T(8,128)(2,1)S(1)}, bf16[896,256]{1,0:T(8,128)(2,1)S(1)}, u32[]{:S(2)}, u32[]{:S(2)}) collective-permute-start(bf16[896,256]{1,0:T(8,128)(2,1)S(1)} %slice.164), channel_id=1, source_target_pairs={{0,8},{8,16},{16,24},{24,32},{32,40},{40,48},{48,56},{56,64},{64,7... | collective-permute-start | bytes 1376264 | tf_op jit(solution)/shard_map/ppermute | solution.py:173
  54.6 50.7 %copy-start.3 = (bf16[896,256]{1,0:T(8,128)(2,1)}, bf16[896,256]{1,0:T(8,128)(2,1)S(1)}, u32[]{:S(2)}) copy-start(bf16[896,256]{1,0:T(8,128)(2,1)S(1)} %collective-permute-done.4.halo_ref) | copy-start | bytes 1376260
  64.6 54.9 %all-to-all-start.4 = ((bf16[32,128,128]{2,1,0:T(8,128)(2,1)}), bf16[32,128,128]{2,1,0:T(8,128)(2,1)S(1)}, u32[]{:S(2)}, u32[]{:S(2)}) async-start(bf16[32,128,128]{2,1,0:T(8,128)(2,1)} %attend.5), calls=%async_computation.4 | async-start | bytes 2097152 | tf_op jit(solution)/shard_map/all_to_all | solution.py:203
  83.2 4.8 %collective-permute-start.5 = (bf16[4,256,256]{2,1,0:T(8,128)(2,1)}, bf16[4,256,256]{2,1,0:T(8,128)(2,1)}, u32[]{:S(2)}, u32[]{:S(2)}) collective-permute-start(bf16[4,256,256]{2,1,0:T(8,128)(2,1)} %get-tuple-element.18), channel_id=1, source_target_pairs={{0,1},{1,0},{2,3},{3,2},{4,5},{5,4},{6,7},{7,6},{8,9},{9,8},{10,11... | collective-permute-start | bytes 1572872 | tf_op jit(solution)/shard_map/ppermute | solution.py:156
  89.3 9.2 %collective-permute-start.6 = (bf16[2,256,256]{2,1,0:T(8,128)(2,1)S(1)}, bf16[2,256,256]{2,1,0:T(8,128)(2,1)S(1)}, u32[]{:S(2)}, u32[]{:S(2)}) collective-permute-start(bf16[2,256,256]{2,1,0:T(8,128)(2,1)S(1)} %get-tuple-element.16), channel_id=1, source_target_pairs={{0,2},{1,3},{2,4},{3,5},{4,6},{5,7},{6,0},{7,1},{8,10},{9,11},{10,... | collective-permute-start | bytes 786440 | tf_op jit(solution)/shard_map/ppermute | solution.py:164
  90.7 14.5 %collective-permute-start.7 = (bf16[2,256,256]{2,1,0:T(8,128)(2,1)S(1)}, bf16[2,256,256]{2,1,0:T(8,128)(2,1)S(1)}, u32[]{:S(2)}, u32[]{:S(2)}) collective-permute-start(bf16[2,256,256]{2,1,0:T(8,128)(2,1)S(1)} %get-tuple-element.15), channel_id=1, source_target_pairs={{0,4},{1,5},{2,6},{3,7},{4,0},{5,1},{6,2},{7,3},{8,12},{9,13},{10,... | collective-permute-start | bytes 786440 | tf_op jit(solution)/shard_map/ppermute | solution.py:164
  93.1 12.1 %collective-permute-start.8 = (bf16[2,256,256]{2,1,0:T(8,128)(2,1)S(1)}, bf16[2,256,256]{2,1,0:T(8,128)(2,1)S(1)}, u32[]{:S(2)}, u32[]{:S(2)}) collective-permute-start(bf16[2,256,256]{2,1,0:T(8,128)(2,1)S(1)} %get-tuple-element.14), channel_id=1, source_target_pairs={{0,6},{1,7},{2,0},{3,1},{4,2},{5,3},{6,4},{7,5},{8,14},{9,15},{10,... | collective-permute-start | bytes 786440 | tf_op jit(solution)/shard_map/ppermute | solution.py:164
  119.5 1.0 copy-start.1
  120.4 85.4 %all-to-all-start.3 = ((bf16[32,128,256]{2,1,0:T(8,128)(2,1)}), bf16[32,128,256]{2,1,0:T(8,128)(2,1)S(1)}, u32[]{:S(2)}, u32[]{:S(2)}) async-start(bf16[32,128,256]{2,1,0:T(8,128)(2,1)} %attend.4), calls=%async_computation.3 | async-start | bytes 4194304 | tf_op jit(solution)/shard_map/all_to_all | solution.py:203
  140.5 4.3 %collective-permute-start = (bf16[4,256,640]{2,1,0:T(8,128)(2,1)S(1)}, bf16[4,256,640]{2,1,0:T(8,128)(2,1)S(1)}, u32[]{:S(2)}, u32[]{:S(2)}) collective-permute-start(bf16[4,256,640]{2,1,0:T(8,128)(2,1)S(1)} %get-tuple-element.12), channel_id=1, source_target_pairs={{0,1},{1,0},{2,3},{3,2},{4,5},{5,4},{6,7},{7,6},{8,9},{9,8},{10,11... | collective-permute-start | bytes 3932168 | tf_op jit(solution)/shard_map/ppermute | solution.py:156
  145.3 17.2 %collective-permute-start.1 = (bf16[2,256,640]{2,1,0:T(8,128)(2,1)S(1)}, bf16[2,256,640]{2,1,0:T(8,128)(2,1)S(1)}, u32[]{:S(2)}, u32[]{:S(2)}) collective-permute-start(bf16[2,256,640]{2,1,0:T(8,128)(2,1)S(1)} %get-tuple-element.10), channel_id=1, source_target_pairs={{0,2},{1,3},{2,4},{3,5},{4,6},{5,7},{6,0},{7,1},{8,10},{9,11},{10,... | collective-permute-start | bytes 1966088 | tf_op jit(solution)/shard_map/ppermute | solution.py:164
  146.4 30.6 %collective-permute-start.2 = (bf16[2,256,640]{2,1,0:T(8,128)(2,1)S(1)}, bf16[2,256,640]{2,1,0:T(8,128)(2,1)S(1)}, u32[]{:S(2)}, u32[]{:S(2)}) collective-permute-start(bf16[2,256,640]{2,1,0:T(8,128)(2,1)S(1)} %get-tuple-element.9), channel_id=1, source_target_pairs={{0,4},{1,5},{2,6},{3,7},{4,0},{5,1},{6,2},{7,3},{8,12},{9,13},{10,... | collective-permute-start | bytes 1966088 | tf_op jit(solution)/shard_map/ppermute | solution.py:164
  148.5 28.5 %collective-permute-start.3 = (bf16[2,256,640]{2,1,0:T(8,128)(2,1)S(1)}, bf16[2,256,640]{2,1,0:T(8,128)(2,1)S(1)}, u32[]{:S(2)}, u32[]{:S(2)}) collective-permute-start(bf16[2,256,640]{2,1,0:T(8,128)(2,1)S(1)} %get-tuple-element.8), channel_id=1, source_target_pairs={{0,6},{1,7},{2,0},{3,1},{4,2},{5,3},{6,4},{7,5},{8,14},{9,15},{10,... | collective-permute-start | bytes 1966088 | tf_op jit(solution)/shard_map/ppermute | solution.py:164
  177.0 1.0 copy-start.4
  203.5 2.3 copy-start
  205.9 10.1 %copy-start.2 = (bf16[32,128,128]{2,1,0:T(8,128)(2,1)S(1)}, bf16[32,128,128]{2,1,0:T(8,128)(2,1)}, u32[]{:S(2)}) copy-start(bf16[32,128,128]{2,1,0:T(8,128)(2,1)} %copy-done.1) | copy-start | bytes 3145732
  205.9 128.4 %all-to-all-start.1 = ((bf16[32,128,640]{2,1,0:T(8,128)(2,1)}), bf16[32,128,640]{2,1,0:T(8,128)(2,1)}, u32[]{:S(2)}, u32[]{:S(2)}) async-start(bf16[32,128,640]{2,1,0:T(8,128)(2,1)} %copy-done), calls=%async_computation.1 | async-start | bytes 10485760 | tf_op jit(solution)/shard_map/all_to_all | solution.py:203

commit v3 on v2

--- a/solution.py
+++ b/solution.py
@@ -16,15 +16,16 @@
 EXP2_SCALE = math.log2(math.e) / math.sqrt(HD)
 
 
-def attend_kernel(
-    doc_ref, slot_ref, origin_ref, shard_ref, q_ref, own_ref, halo_ref, out_ref, win_ref, *, heads, count
-):
-    index = pl.program_id(0)
-
-    @pl.when(index == 0)
+def attend_kernel(doc_ref, slot_ref, origin_ref, shard_ref, q_ref, *refs, heads, count, base, ahead):
+    own_ref, win_ref, out_ref = refs[0], refs[-1], refs[-2]
+    step = pl.program_id(0)
+    index = base + step
+
+    @pl.when(step == 0)
     def _():
-        win_ref[: HALO * BLK, :] = halo_ref[...]
-        win_ref[HALO * BLK :, :] = own_ref[...]
+        if ahead:
+            win_ref[: ahead * BLK, :] = refs[1][...]
+        win_ref[ahead * BLK :, :] = own_ref[...]
 
     block = shard_ref[0] * count + index
     doc = doc_ref[block]
@@ -38,7 +39,7 @@
     causal = column <= row
 
     def with_tiles(n):
-        start = pl.multiple_of((index + MAXDOC - n) * BLK, BLK)
+        start = pl.multiple_of((index + ahead + 1 - n) * BLK, BLK)
         keys = win_ref[pl.ds(start, n * BLK), :HD]
         values = win_ref[pl.ds(start, n * BLK), HD:]
         for head in range(heads):
@@ -61,32 +62,98 @@
         pl.when(tiles == n)(functools.partial(with_tiles, n))
 
 
-def attend(queries, kv_own, kv_halo, doc_ids, slot, origin, shard, slots):
-    rows, width = queries.shape
-    count = rows // BLK
-    heads = width // HD
+def attend(queries, q_column, heads, own, halo, tables, count, slots, base=0, steps=None, result=None):
+    doc_ids, slot, origin, shard = tables
+    steps = count if steps is None else steps
+    width = heads * HD
+    ahead = 0 if halo is None else HALO
+    own_blocks = base + steps
+    given = [queries, own] + ([] if halo is None else [halo]) + ([] if result is None else [result])
+    in_specs = [
+        pl.BlockSpec((BLK, width), lambda i, doc, slot, origin, shard: (origin[base + i], q_column)),
+        pl.BlockSpec((own_blocks * BLK, 2 * HD), lambda i, *_: (0, 0)),
+    ]
+    if halo is not None:
+        in_specs.append(pl.BlockSpec(halo.shape, lambda i, *_: (0, 0)))
+    if result is not None:
+        in_specs.append(pl.BlockSpec(memory_space=pl.ANY))
     return pl.pallas_call(
-        functools.partial(attend_kernel, heads=heads, count=count),
+        functools.partial(attend_kernel, heads=heads, count=count, base=base, ahead=ahead),
         grid_spec=pltpu.PrefetchScalarGridSpec(
             num_scalar_prefetch=4,
-            grid=(count,),
-            in_specs=[
-                pl.BlockSpec((BLK, width), lambda i, doc, slot, origin, shard: (origin[i], 0)),
-                pl.BlockSpec(kv_own.shape, lambda i, doc, slot, origin, shard: (0, 0)),
-                pl.BlockSpec(kv_halo.shape, lambda i, doc, slot, origin, shard: (0, 0)),
-            ],
-            out_specs=pl.BlockSpec((1, BLK, width), lambda i, doc, slot, origin, shard: (slot[i], 0, 0)),
-            scratch_shapes=[pltpu.VMEM((kv_own.shape[0] + kv_halo.shape[0], 2 * HD), jnp.bfloat16)],
+            grid=(steps,),
+            in_specs=in_specs,
+            out_specs=pl.BlockSpec((1, BLK, width), lambda i, doc, slot, origin, shard: (slot[base + i], 0, 0)),
+            scratch_shapes=[pltpu.VMEM(((own_blocks + ahead) * BLK, 2 * HD), jnp.bfloat16)],
         ),
         out_shape=jax.ShapeDtypeStruct((slots, BLK, width), jnp.bfloat16),
+        input_output_aliases={} if result is None else {4 + len(given) - 1: 0},
         compiler_params=pltpu.CompilerParams(vmem_limit_bytes=32 * 1024 * 1024),
         cost_estimate=pl.CostEstimate(
-            flops=4 * rows * heads * HD * BLK * 4,
-            bytes_accessed=4 * rows * width + 4 * kv_own.size,
-            transcendentals=rows * heads * BLK * 4,
+            flops=4 * steps * BLK * heads * HD * BLK * 4,
+            bytes_accessed=4 * steps * BLK * width + 4 * own_blocks * BLK * HD,
+            transcendentals=steps * BLK * heads * BLK * 4,
         ),
         name="attend",
-    )(doc_ids, slot, origin, shard, queries, kv_own, kv_halo)
+    )(doc_ids, slot, origin, shard, *given)
+
+
+def first_parts_kernel(k_ref, v_ref, q_ref, out_ref):
+    width = k_ref.shape[1]
+    out_ref[0, :, :width] = k_ref[...]
+    out_ref[0, :, width : 2 * width] = v_ref[...]
+    out_ref[0, :, 2 * width :] = q_ref[...]
+
+
+def first_parts(key, value, query, head_count, width):
+    rows = query.shape[0]
+    kv_width, q_width = key.shape[1] // head_count, query.shape[1] // head_count
+    return pl.pallas_call(
+        first_parts_kernel,
+        grid=(head_count,),
+        in_specs=[
+            pl.BlockSpec((rows, kv_width), lambda h: (0, h)),
+            pl.BlockSpec((rows, kv_width), lambda h: (0, h)),
+            pl.BlockSpec((rows, width), lambda h: (0, h * (q_width // width))),
+        ],
+        out_specs=pl.BlockSpec((1, rows, 2 * kv_width + width), lambda h: (h, 0, 0)),
+        out_shape=jax.ShapeDtypeStruct((head_count, rows, 2 * kv_width + width), jnp.bfloat16),
+        name="first_parts",
+    )(key, value, query)
+
+
+def later_parts_kernel(place_ref, q_ref, *out_refs, firsts):
+    core = place_ref[0]
+    pairs = len(firsts)
+
+    def write(refs):
+        for ref, first in zip(refs, firsts):
+            ref[0] = q_ref[:, first : first + ref.shape[2]]
+
+    same = pl.program_id(0) % 2 == core
+    pl.when(same)(lambda: write(out_refs[:pairs]))
+    pl.when(jnp.logical_not(same))(lambda: write(out_refs[pairs:]))
+
+
+def later_parts(query, place, head_count, firsts, widths):
+    rows, q_width, chips = query.shape[0], query.shape[1] // head_count, head_count // 2
+    specs = [
+        pl.BlockSpec((1, rows, width), lambda h, place: ((h // 2 + chips - place[1]) % chips, 0, 0))
+        for width in widths
+    ]
+    shapes = [jax.ShapeDtypeStruct((chips, rows, width), jnp.bfloat16) for width in widths]
+    outs = pl.pallas_call(
+        functools.partial(later_parts_kernel, firsts=firsts),
+        grid_spec=pltpu.PrefetchScalarGridSpec(
+            num_scalar_prefetch=1,
+            grid=(head_count,),
+            in_specs=[pl.BlockSpec((rows, q_width), lambda h, place: (0, h))],
+            out_specs=specs + specs,
+        ),
+        out_shape=shapes + shapes,
+        name="later_parts",
+    )(place, query)
+    return outs[: len(widths)], outs[len(widths) :]
 
 
 def place_kernel(source_ref, *refs, count, first, width):
@@ -137,41 +204,16 @@
     count = rows // BLK
     per_device = local_rows // BLK
     q_width = query.shape[1] // head_count
-    kv_width = key.shape[1] // head_count
     shard = lax.axis_index("ctx").astype(jnp.int32)
     member = lax.axis_index("head").astype(jnp.int32)
     core, chip, chips = member % 2, member // 2, head_count // 2
 
-    def by_head(array, width, first, size):
-        return jnp.stack([array[:, h * width + first : h * width + first + size] for h in range(head_count)])
-
-    def exchange(parts):
-        moved = lax.all_to_all(parts, "head", split_axis=0, concat_axis=0, tiled=True)
-        return moved.reshape(rows, parts.shape[2])
-
-    def core_swap(parts):
-        pairs = parts.reshape(chips, 2, local_rows, parts.shape[2])
-        kept = lax.dynamic_index_in_dim(pairs, core, 1, False)
-        given = lax.dynamic_index_in_dim(pairs, 1 - core, 1, False)
-        got = lax.ppermute(given, "head", [(h, h ^ 1) for h in range(head_count)])
-        return jnp.stack([kept, got], axis=1)
-
-    def chip_exchange(both):
-        arrived = []
-        for step in range(chips):
-            piece = lax.dynamic_index_in_dim(both, (chip + step) % chips, 0, False)
-            if step:
-                piece = lax.ppermute(
-                    piece, "head", [(h, (h + 2 * step) % head_count) for h in range(head_count)]
-                )
-            arrived.append(piece)
-        return jnp.stack(arrived).reshape(rows, both.shape[3])
-
-    kv_own = exchange(
-        jnp.concatenate([by_head(key, kv_width, 0, kv_width), by_head(value, kv_width, 0, kv_width)], axis=2)
-    )
-    kv_halo = lax.ppermute(
-        kv_own[rows - HALO * BLK :], "ctx", [(i, i + 1) for i in range(shard_count - 1)]
+    widths = [heads * HD for heads in CHUNKS]
+    firsts = [sum(widths[:i]) for i in range(len(widths))]
+    kept, given = later_parts(query, jnp.stack([core, chip]), head_count, firsts[1:], widths[1:])
+    got = [lax.ppermute(part, "head", [(h, h ^ 1) for h in range(head_count)]) for part in given]
+    opening = lax.all_to_all(
+        first_parts(key, value, query, head_count, widths[0]), "head", split_axis=0, concat_axis=0, tiled=True
     )
 
     index = jnp.arange(count, dtype=jnp.int32)
@@ -185,24 +227,37 @@
     steps_back = (chip - giver // 2 + chips) % chips
     arrival = (steps_back * 2 + jnp.where(giver % 2 == core, 0, 1)) * per_device + index % per_device
 
+    opening, kept, got, target, source, arrival = lax.optimization_barrier(
+        (opening, kept, got, target, source, arrival)
+    )
+    opening = opening.reshape(rows, 2 * HD + widths[0])
+    halo = lax.ppermute(
+        opening[rows - HALO * BLK :, : 2 * HD], "ctx", [(i, i + 1) for i in range(shard_count - 1)]
+    )
+    straight = (doc_ids, target, index, shard.reshape(1))
+    arranged = (doc_ids, target, arrival, shard.reshape(1))
+
     result = None
-    first = 0
-    earlier = kv_own
     for turn, heads in enumerate(CHUNKS):
-        width = heads * HD
-        parts = by_head(query, q_width, first, width)
         if turn == 0:
-            queries = exchange(parts)
-            origin = index
+            column = 2 * HD // widths[0]
+            sent = attend(
+                opening, column, heads, opening, None, straight, count, shard_count, HALO, count - HALO
+            )
+            sent = attend(opening, column, heads, opening, halo, straight, count, shard_count, 0, HALO, sent)
         else:
-            both, earlier = lax.optimization_barrier((core_swap(parts), earlier))
-            queries = chip_exchange(both)
-            origin = arrival
-        sent = attend(queries, kv_own, kv_halo, doc_ids, target, origin, shard.reshape(1), shard_count)
-        earlier = queries if turn == 0 else earlier
+            arrived = []
+            for step in range(chips):
+                piece = jnp.stack([kept[turn - 1][step], got[turn - 1][step]])
+                if step:
+                    piece = lax.ppermute(
+                        piece, "head", [(h, (h + 2 * step) % head_count) for h in range(head_count)]
+                    )
+                arrived.append(piece)
+            queries = jnp.stack(arrived).reshape(rows, widths[turn])
+            sent = attend(queries, 0, heads, opening, halo, arranged, count, shard_count)
         received = lax.all_to_all(sent, "ctx", split_axis=0, concat_axis=0, tiled=True)
-        result = place(received, source, result, first, count, q_width)
-        first += width
+        result = place(received, source, result, firsts[turn], count, q_width)
     return result
 
 

time: 342 us -> 299 us (0.87)
  local copies, waits for them, and re-layouts: 59.3 us -> 7.81 us
  Pallas kernels: 58.4 us -> 72.1 us
  starting transfers between devices: 57.4 us -> 47.3 us
  waiting for transfers between devices: 159 us -> 165 us
    unnamed x49 -> x14, local copies, waits for them, and re-layouts: 49.2 us -> 3.91 us
    pallas_call x3 -> x6, Pallas kernels: 49.5 us -> 63.8 us  [the longest x4 51 us: attend(): pl.pallas_call(functools.partial(attend_kernel, heads=heads, count=count,...]
    all_to_all x2 -> x1, waiting for transfers between devices: 2.74 us -> 8.75 us  [shards(): lax.all_to_all(first_parts(key, value, query, head_count, widths[0]), 'he...]
    another operation x4 -> x0, local copies, waits for them, and re-layouts: 5.66 us -> none  [by_head(): jnp.stack([array[:, h * width + first:h * width + first + size] for h in...]
    all_to_all x2 -> x1, starting transfers between devices: 9.95 us -> 5.14 us  [shards(): lax.all_to_all(first_parts(key, value, query, head_count, widths[0]), 'he...]
    dynamic_slice x4 -> x0, local copies, waits for them, and re-layouts: 4.36 us -> none  [the longest x2 4.04 us: core_swap(): kept = lax.dynamic_index_in_dim(pairs, core, 1, False)]
    ppermute x9, starting transfers between devices: 16.1 us -> 11.9 us  [the longest x6 7.84 us: shards(): lax.ppermute(piece, 'head', [(h, (h + 2 * step) % head_count) for h in ra...]
    slice x1 -> x5, local copies, waits for them, and re-layouts: 0.03 us -> 3.9 us  [the longest x4 3.87 us: shards(): piece = jnp.stack([kept[turn - 1][step], got[turn - 1][step]])]
  transfers between devices with their start and end apart: 14 -> 13, of which waited for: 8 -> 10; matrix products, arithmetic and copies ran while one was open for 13% -> 2% of each run, Pallas kernels for 13% -> 20%
where the time goes in v3:
time: 299 us; the launch traced here: 295 us
  waiting for transfers between devices  165 us (55%)
  Pallas kernels  72.1 us (24%)
  starting transfers between devices  47.3 us (16%)
  local copies, waits for them, and re-layouts  7.81 us (3%)
    all_to_all x3, waiting for transfers between devices, shards(): lax.all_to_all(sent, 'ctx', split_axis=0, concat_axis=0, tiled=True)  111 us
    pallas_call x4, Pallas kernels, attend(): pl.pallas_call(functools.partial(attend_kernel, heads=heads, count=count,...  51 us
    ppermute x6, waiting for transfers between devices, shards(): lax.ppermute(piece, 'head', [(h, (h + 2 * step) % head_count) for h in ra...  38.9 us
    all_to_all x3, starting transfers between devices, shards(): lax.all_to_all(sent, 'ctx', split_axis=0, concat_axis=0, tiled=True)  30.3 us
    all_to_all x1, waiting for transfers between devices, shards(): lax.all_to_all(first_parts(key, value, query, head_count, widths[0]), 'he...  8.75 us
    pallas_call x3, Pallas kernels, place(): pl.pallas_call(functools.partial(place_kernel, count=count, first=first,...  8.36 us
    ppermute x6, starting transfers between devices, shards(): lax.ppermute(piece, 'head', [(h, (h + 2 * step) % head_count) for h in ra...  7.84 us
    pallas_call x1, Pallas kernels, later_parts(): pl.pallas_call(functools.partial(later_parts_kernel, firsts=firsts), grid...  7.37 us
  transfers between devices with their start and end apart: 13, of which 10 were waited for; matrix products, arithmetic and copies ran while one was open for 2% of the time, Pallas kernels for 20%

profile of v3, /device:TPU:33, one launch (start us, length us, event | category | flops | bytes accessed | tf_op | source)
XLA Modules:
  0.0 294.6 jit_solution(14703296580685733799)
XLA Ops:
  0.0 5.4 %first_parts.1 = bf16[8,256,384]{2,1,0:T(8,128)(2,1)} custom-call(bf16[256,1024]{1,0:T(8,128)(2,1)} %k_ref.1, bf16[256,1024]{1,0:T(8,128)(2,1)} %v_ref.1, bf16[256,8192]{1,0:T(8,128)(2,1)} %q_ref.3), custom_call_target="tpu_custom_call" | custom-call | tf_op jit(solution)/shard_map/first_parts/pallas_call | solution.py:111
  5.4 5.1 %all-to-all-start = ((bf16[8,256,384]{2,1,0:T(8,128)(2,1)}), bf16[8,256,384]{2,1,0:T(8,128)(2,1)S(1)}, u32[]{:S(2)}, u32[]{:S(2)}) async-start(bf16[8,256,384]{2,1,0:T(8,128)(2,1)} %first_parts.1), calls=%async_computation | async-start | bytes 3145728 | tf_op jit(solution)/shard_map/all_to_all | solution.py:215
  10.6 0.6 pad_add_fusion.place_ref
  11.1 7.4 %later_parts.1 = (bf16[4,256,256]{2,1,0:T(8,128)(2,1)}, bf16[4,256,640]{2,1,0:T(8,128)(2,1)}, bf16[4,256,256]{2,1,0:T(8,128)(2,1)}, bf16[4,256,640]{2,1,0:T(8,128)(2,1)}) custom-call(s32[2]{0:T(128)} %pad_add_fusion.place_ref, bf16[256,8192]{1,0:T(8,128)(2,1)} %q_ref.3), custom_call_target="tpu_custom_call" | custom-call | tf_op jit(solution)/shard_map/later_parts/pallas_call | solution.py:145
  18.5 0.0 collective-permute-start.1
  18.5 0.5 collective-permute-start
  19.0 0.1 and_select_fusion.5
  19.1 0.2 select_reduce_fusion.slot_ref
  19.3 3.2 %collective-permute-done = bf16[4,256,256]{2,1,0:T(8,128)(2,1)S(1)} collective-permute-done((bf16[4,256,256]{2,1,0:T(8,128)(2,1)}, bf16[4,256,256]{2,1,0:T(8,128)(2,1)S(1)}, u32[]{:S(2)}, u32[]{:S(2)}) %collective-permute-start) | collective-permute-done | bytes 524320 | tf_op jit(solution)/shard_map/ppermute | solution.py:214
  22.5 8.8 %all-to-all-done = bf16[8,256,384]{2,1,0:T(8,128)(2,1)S(1)} async-done(((bf16[8,256,384]{2,1,0:T(8,128)(2,1)}), bf16[8,256,384]{2,1,0:T(8,128)(2,1)S(1)}, u32[]{:S(2)}, u32[]{:S(2)}) %all-to-all-start) | async-done | bytes 1572896 | tf_op jit(solution)/shard_map/all_to_all | solution.py:215
  31.3 3.5 %collective-permute-start.5 = (bf16[896,256]{1,0:T(8,128)(2,1)S(1)}, bf16[896,256]{1,0:T(8,128)(2,1)S(1)}, u32[]{:S(2)}, u32[]{:S(2)}) collective-permute-start(bf16[896,256]{1,0:T(8,128)(2,1)S(1)} %slice.68), channel_id=1, source_target_pairs={{0,8},{8,16},{16,24},{24,32},{32,40},{40,48},{48,56},{56,64},{64,7... | collective-permute-start | bytes 1376264 | tf_op jit(solution)/shard_map/ppermute | solution.py:234
  34.9 6.4 %attend.6.refs_2_ = bf16[32,128,128]{2,1,0:T(8,128)(2,1)} custom-call(s32[512]{0:T(512)S(1)} %copy-done.2, s32[16]{0:T(128)S(1)} %select_reduce_fusion.slot_ref, s32[16]{0:T(128)S(1)} %iota.24.origin_ref, s32[1]{0:T(128)} %bitcast.2.shard_ref, bf16[2048,384]{1,0:T(8,128)(2,1)S(1)} %bitcast.17, bf16[2048,384]{1,0:T(8,128)(2,1)S(1)} %bitcast.18), custom_call_target="tpu_custom_call" | custom-call | flops 301989888 | bytes 1638400 | tf_op jit(solution)/shard_map/attend/pallas_call | solution.py:80
  41.2 3.1 %collective-permute-done.5.refs_1_ = bf16[896,256]{1,0:T(8,128)(2,1)S(1)} collective-permute-done((bf16[896,256]{1,0:T(8,128)(2,1)S(1)}, bf16[896,256]{1,0:T(8,128)(2,1)S(1)}, u32[]{:S(2)}, u32[]{:S(2)}) %collective-permute-start.5) | collective-permute-done | bytes 458784 | tf_op jit(solution)/shard_map/ppermute | solution.py:234
  44.4 5.2 %attend.7 = bf16[32,128,128]{2,1,0:T(8,128)(2,1)} custom-call(s32[512]{0:T(512)S(1)} %copy-done.2, s32[16]{0:T(128)S(1)} %select_reduce_fusion.slot_ref, s32[16]{0:T(128)S(1)} %iota.23.origin_ref, s32[1]{0:T(128)} %bitcast.2.shard_ref, bf16[2048,384]{1,0:T(8,128)(2,1)S(1)} %bitcast.19, ...), custom_call_target="tpu_custom_call", output_to_operand_aliasing={{}: (7, {})} | custom-call | flops 234881024 | bytes 917504 | tf_op jit(solution)/shard_map/attend/pallas_call | solution.py:80
  49.6 11.8 %all-to-all-start.3 = ((bf16[32,128,128]{2,1,0:T(8,128)(2,1)}), bf16[32,128,128]{2,1,0:T(8,128)(2,1)S(1)}, u32[]{:S(2)}, u32[]{:S(2)}) async-start(bf16[32,128,128]{2,1,0:T(8,128)(2,1)} %attend.7), calls=%async_computation.3 | async-start | bytes 2097152 | tf_op jit(solution)/shard_map/all_to_all | solution.py:259
  61.4 1.1 fusion.9
  62.5 1.1 fusion.10
  63.7 0.4 collective-permute-start.6
  64.1 1.9 collective-permute-start.7
  66.0 0.8 collective-permute-start.8
  66.8 4.9 %collective-permute-done.6 = bf16[2,256,256]{2,1,0:T(8,128)(2,1)S(1)} collective-permute-done((bf16[2,256,256]{2,1,0:T(8,128)(2,1)S(1)}, bf16[2,256,256]{2,1,0:T(8,128)(2,1)S(1)}, u32[]{:S(2)}, u32[]{:S(2)}) %collective-permute-start.6) | collective-permute-done | bytes 262176 | tf_op jit(solution)/shard_map/ppermute | solution.py:253
  71.7 3.5 %collective-permute-done.7 = bf16[2,256,256]{2,1,0:T(8,128)(2,1)S(1)} collective-permute-done((bf16[2,256,256]{2,1,0:T(8,128)(2,1)S(1)}, bf16[2,256,256]{2,1,0:T(8,128)(2,1)S(1)}, u32[]{:S(2)}, u32[]{:S(2)}) %collective-permute-start.7) | collective-permute-done | bytes 262176 | tf_op jit(solution)/shard_map/ppermute | solution.py:253
  75.3 3.0 %collective-permute-done.8 = bf16[2,256,256]{2,1,0:T(8,128)(2,1)S(1)} collective-permute-done((bf16[2,256,256]{2,1,0:T(8,128)(2,1)S(1)}, bf16[2,256,256]{2,1,0:T(8,128)(2,1)S(1)}, u32[]{:S(2)}, u32[]{:S(2)}) %collective-permute-start.8) | collective-permute-done | bytes 262176 | tf_op jit(solution)/shard_map/ppermute | solution.py:253
  78.3 0.1 pad_maximum_fusion.1
  78.4 13.6 %attend.5 = bf16[32,128,256]{2,1,0:T(8,128)(2,1)S(1)} custom-call(s32[512]{0:T(512)S(1)} %copy-done.2, s32[16]{0:T(128)S(1)} %select_reduce_fusion.slot_ref, s32[16]{0:T(128)S(1)} %get-tuple-element.23.origin_ref, s32[1]{0:T(128)} %bitcast.2.shard_ref, bf16[2048,256]{1,0:T(8,128)(2,1)S(1)} %bitcast.23, bf16[2048,384]{1,0:T(8,128)(2,1)S(1)} %bitcast.21, ...), custom_call_target="tpu_custom_call" | custom-call | flops 1073741824 | bytes 3145728 | tf_op jit(solution)/shard_map/attend/pallas_call | solution.py:80
  92.0 1.3 copy-done
  93.3 9.4 %all-to-all-start.2 = ((bf16[32,128,256]{2,1,0:T(8,128)(2,1)}), bf16[32,128,256]{2,1,0:T(8,128)(2,1)}, u32[]{:S(2)}, u32[]{:S(2)}) async-start(bf16[32,128,256]{2,1,0:T(8,128)(2,1)} %copy-done), calls=%async_computation.2 | async-start | bytes 4194304 | tf_op jit(solution)/shard_map/all_to_all | solution.py:259
  102.7 1.5 fusion.7
  104.2 0.2 copy-done.4
  104.4 0.1 fusion.8
  104.5 0.1 pad_maximum_fusion.2
  104.6 0.4 collective-permute-start.2
  105.0 0.1 pad_maximum_fusion.3
  105.1 4.3 %collective-permute-start.3 = (bf16[2,256,640]{2,1,0:T(8,128)(2,1)S(1)}, bf16[2,256,640]{2,1,0:T(8,128)(2,1)S(1)}, u32[]{:S(2)}, u32[]{:S(2)}) collective-permute-start(bf16[2,256,640]{2,1,0:T(8,128)(2,1)S(1)} %pad_maximum_fusion.3), channel_id=1, source_target_pairs={{0,4},{1,5},{2,6},{3,7},{4,0},{5,1},{6,2},{7,3},{8,12},{9,13},{10,... | collective-permute-start | bytes 1966088 | tf_op jit(solution)/shard_map/ppermute | solution.py:253
  109.5 0.1 pad_maximum_fusion.4
  109.5 0.1 collective-permute-start.4
  109.6 0.1 maximum_bitcast_fusion
  109.7 11.7 %collective-permute-done.2 = bf16[2,256,640]{2,1,0:T(8,128)(2,1)S(1)} collective-permute-done((bf16[2,256,640]{2,1,0:T(8,128)(2,1)S(1)}, bf16[2,256,640]{2,1,0:T(8,128)(2,1)S(1)}, u32[]{:S(2)}, u32[]{:S(2)}) %collective-permute-start.2) | collective-permute-done | bytes 655392 | tf_op jit(solution)/shard_map/ppermute | solution.py:253
  121.4 15.7 %collective-permute-done.3 = bf16[2,256,640]{2,1,0:T(8,128)(2,1)S(1)} collective-permute-done((bf16[2,256,640]{2,1,0:T(8,128)(2,1)S(1)}, bf16[2,256,640]{2,1,0:T(8,128)(2,1)S(1)}, u32[]{:S(2)}, u32[]{:S(2)}) %collective-permute-start.3) | collective-permute-done | bytes 655392 | tf_op jit(solution)/shard_map/ppermute | solution.py:253
  137.0 0.1 collective-permute-done.4
  137.1 0.4 pad_maximum_fusion
  137.5 25.9 %attend.4 = bf16[32,128,640]{2,1,0:T(8,128)(2,1)S(1)} custom-call(s32[512]{0:T(512)S(1)} %copy-done.2, s32[16]{0:T(128)S(1)} %select_reduce_fusion.slot_ref, s32[16]{0:T(128)S(1)} %get-tuple-element.23.origin_ref, s32[1]{0:T(128)} %bitcast.2.shard_ref, bf16[2048,640]{1,0:T(8,128)(2,1)S(1)} %bitcast.24, bf16[2048,384]{1,0:T(8,128)(2,1)S(1)} %bitcast.22, ...), custom_call_target="tpu_custom_call" | custom-call | flops 2684354560 | bytes 6291456 | tf_op jit(solution)/shard_map/attend/pallas_call | solution.py:80
  163.4 2.4 copy-done.1
  165.7 9.1 %all-to-all-start.1 = ((bf16[32,128,640]{2,1,0:T(8,128)(2,1)}), bf16[32,128,640]{2,1,0:T(8,128)(2,1)}, u32[]{:S(2)}, u32[]{:S(2)}) async-start(bf16[32,128,640]{2,1,0:T(8,128)(2,1)} %copy-done.1), calls=%async_computation.1 | async-start | bytes 10485760 | tf_op jit(solution)/shard_map/all_to_all | solution.py:259
  174.8 2.3 place.3.refs_1_
  177.1 2.7 place.4.refs_1_
  179.9 111.2 %all-to-all-done.1.refs_0_ = bf16[32,128,640]{2,1,0:T(8,128)(2,1)} async-done(((bf16[32,128,640]{2,1,0:T(8,128)(2,1)}), bf16[32,128,640]{2,1,0:T(8,128)(2,1)}, u32[]{:S(2)}, u32[]{:S(2)}) %all-to-all-start.1) | async-done | bytes 5242912 | tf_op jit(solution)/shard_map/all_to_all | solution.py:259
  291.1 3.3 %place.5 = bf16[2048,1024]{1,0:T(8,128)(2,1)} custom-call(s32[16]{0:T(128)S(1)} %get-tuple-element.21.source_ref, bf16[32,128,640]{2,1,0:T(8,128)(2,1)} %all-to-all-done.1.refs_0_, bf16[2048,1024]{1,0:T(8,128)(2,1)} %place.4.refs_1_), custom_call_target="tpu_custom_call", output_to_operand_aliasing={{}: (2, {})} | custom-call | bytes 5242880 | tf_op jit(solution)/shard_map/place/pallas_call | solution.py:182
  (23 shorter events, 0.2 us)
Async XLA Ops:
  5.4 25.9 %all-to-all-start = ((bf16[8,256,384]{2,1,0:T(8,128)(2,1)}), bf16[8,256,384]{2,1,0:T(8,128)(2,1)S(1)}, u32[]{:S(2)}, u32[]{:S(2)}) async-start(bf16[8,256,384]{2,1,0:T(8,128)(2,1)} %first_parts.1), calls=%async_computation | async-start | bytes 3145728 | tf_op jit(solution)/shard_map/all_to_all | solution.py:215
  10.6 8.5 %copy-start.6 = (s32[512]{0:T(512)S(1)}, s32[512]{0:T(512)}, u32[]{:S(2)}) copy-start(s32[512]{0:T(512)} %param.9) | copy-start | bytes 6148
  10.6 24.3 %copy-start.2 = (s32[512]{0:T(512)S(1)}, s32[512]{0:T(512)}, u32[]{:S(2)}) copy-start(s32[512]{0:T(512)} %doc_ref.7) | copy-start | bytes 6148
  18.5 4.0 %collective-permute-start.1 = (bf16[4,256,640]{2,1,0:T(8,128)(2,1)}, bf16[4,256,640]{2,1,0:T(8,128)(2,1)S(1)}, u32[]{:S(2)}, u32[]{:S(2)}) collective-permute-start(bf16[4,256,640]{2,1,0:T(8,128)(2,1)} %get-tuple-element.20), channel_id=1, source_target_pairs={{0,1},{1,0},{2,3},{3,2},{4,5},{5,4},{6,7},{7,6},{8,9},{9,8},{10,11... | collective-permute-start | bytes 3932168 | tf_op jit(solution)/shard_map/ppermute | solution.py:214
  18.5 4.0 %collective-permute-start = (bf16[4,256,256]{2,1,0:T(8,128)(2,1)}, bf16[4,256,256]{2,1,0:T(8,128)(2,1)S(1)}, u32[]{:S(2)}, u32[]{:S(2)}) collective-permute-start(bf16[4,256,256]{2,1,0:T(8,128)(2,1)} %get-tuple-element.19), channel_id=1, source_target_pairs={{0,1},{1,0},{2,3},{3,2},{4,5},{5,4},{6,7},{7,6},{8,9},{9,8},{10,11... | collective-permute-start | bytes 1572872 | tf_op jit(solution)/shard_map/ppermute | solution.py:214
  22.5 27.1 %copy-start.5 = (bf16[4,256,256]{2,1,0:T(8,128)(2,1)}, bf16[4,256,256]{2,1,0:T(8,128)(2,1)S(1)}, u32[]{:S(2)}) copy-start(bf16[4,256,256]{2,1,0:T(8,128)(2,1)S(1)} %collective-permute-done) | copy-start | bytes 1572868
  22.5 8.8 %copy-start.3 = (bf16[4,256,640]{2,1,0:T(8,128)(2,1)}, bf16[4,256,640]{2,1,0:T(8,128)(2,1)S(1)}, u32[]{:S(2)}) copy-start(bf16[4,256,640]{2,1,0:T(8,128)(2,1)S(1)} %collective-permute-done.1) | copy-start | bytes 3932164
  31.3 13.1 %collective-permute-start.5 = (bf16[896,256]{1,0:T(8,128)(2,1)S(1)}, bf16[896,256]{1,0:T(8,128)(2,1)S(1)}, u32[]{:S(2)}, u32[]{:S(2)}) collective-permute-start(bf16[896,256]{1,0:T(8,128)(2,1)S(1)} %slice.68), channel_id=1, source_target_pairs={{0,8},{8,16},{16,24},{24,32},{32,40},{40,48},{48,56},{56,64},{64,7... | collective-permute-start | bytes 1376264 | tf_op jit(solution)/shard_map/ppermute | solution.py:234
  49.6 43.7 %all-to-all-start.3 = ((bf16[32,128,128]{2,1,0:T(8,128)(2,1)}), bf16[32,128,128]{2,1,0:T(8,128)(2,1)S(1)}, u32[]{:S(2)}, u32[]{:S(2)}) async-start(bf16[32,128,128]{2,1,0:T(8,128)(2,1)} %attend.7), calls=%async_computation.3 | async-start | bytes 2097152 | tf_op jit(solution)/shard_map/all_to_all | solution.py:259
  63.7 8.0 %collective-permute-start.6 = (bf16[2,256,256]{2,1,0:T(8,128)(2,1)S(1)}, bf16[2,256,256]{2,1,0:T(8,128)(2,1)S(1)}, u32[]{:S(2)}, u32[]{:S(2)}) collective-permute-start(bf16[2,256,256]{2,1,0:T(8,128)(2,1)S(1)} %pad_maximum_fusion.5), channel_id=1, source_target_pairs={{0,2},{1,3},{2,4},{3,5},{4,6},{5,7},{6,0},{7,1},{8,10},{9,11},{10,... | collective-permute-start | bytes 786440 | tf_op jit(solution)/shard_map/ppermute | solution.py:253
  64.1 11.2 %collective-permute-start.7 = (bf16[2,256,256]{2,1,0:T(8,128)(2,1)S(1)}, bf16[2,256,256]{2,1,0:T(8,128)(2,1)S(1)}, u32[]{:S(2)}, u32[]{:S(2)}) collective-permute-start(bf16[2,256,256]{2,1,0:T(8,128)(2,1)S(1)} %pad_maximum_fusion.6), channel_id=1, source_target_pairs={{0,4},{1,5},{2,6},{3,7},{4,0},{5,1},{6,2},{7,3},{8,12},{9,13},{10,... | collective-permute-start | bytes 786440 | tf_op jit(solution)/shard_map/ppermute | solution.py:253
  66.0 12.3 %collective-permute-start.8 = (bf16[2,256,256]{2,1,0:T(8,128)(2,1)S(1)}, bf16[2,256,256]{2,1,0:T(8,128)(2,1)S(1)}, u32[]{:S(2)}, u32[]{:S(2)}) collective-permute-start(bf16[2,256,256]{2,1,0:T(8,128)(2,1)S(1)} %pad_maximum_fusion.7), channel_id=1, source_target_pairs={{0,6},{1,7},{2,0},{3,1},{4,2},{5,3},{6,4},{7,5},{8,14},{9,15},{10,... | collective-permute-start | bytes 786440 | tf_op jit(solution)/shard_map/ppermute | solution.py:253
  92.0 1.3 copy-start
  93.3 72.4 %all-to-all-start.2 = ((bf16[32,128,256]{2,1,0:T(8,128)(2,1)}), bf16[32,128,256]{2,1,0:T(8,128)(2,1)}, u32[]{:S(2)}, u32[]{:S(2)}) async-start(bf16[32,128,256]{2,1,0:T(8,128)(2,1)} %copy-done), calls=%async_computation.2 | async-start | bytes 4194304 | tf_op jit(solution)/shard_map/all_to_all | solution.py:259
  102.7 1.7 copy-start.4
  104.6 16.7 %collective-permute-start.2 = (bf16[2,256,640]{2,1,0:T(8,128)(2,1)S(1)}, bf16[2,256,640]{2,1,0:T(8,128)(2,1)S(1)}, u32[]{:S(2)}, u32[]{:S(2)}) collective-permute-start(bf16[2,256,640]{2,1,0:T(8,128)(2,1)S(1)} %pad_maximum_fusion.2), channel_id=1, source_target_pairs={{0,2},{1,3},{2,4},{3,5},{4,6},{5,7},{6,0},{7,1},{8,10},{9,11},{10,... | collective-permute-start | bytes 1966088 | tf_op jit(solution)/shard_map/ppermute | solution.py:253
  105.1 31.9 %collective-permute-start.3 = (bf16[2,256,640]{2,1,0:T(8,128)(2,1)S(1)}, bf16[2,256,640]{2,1,0:T(8,128)(2,1)S(1)}, u32[]{:S(2)}, u32[]{:S(2)}) collective-permute-start(bf16[2,256,640]{2,1,0:T(8,128)(2,1)S(1)} %pad_maximum_fusion.3), channel_id=1, source_target_pairs={{0,4},{1,5},{2,6},{3,7},{4,0},{5,1},{6,2},{7,3},{8,12},{9,13},{10,... | collective-permute-start | bytes 1966088 | tf_op jit(solution)/shard_map/ppermute | solution.py:253
  109.5 27.6 %collective-permute-start.4 = (bf16[2,256,640]{2,1,0:T(8,128)(2,1)S(1)}, bf16[2,256,640]{2,1,0:T(8,128)(2,1)S(1)}, u32[]{:S(2)}, u32[]{:S(2)}) collective-permute-start(bf16[2,256,640]{2,1,0:T(8,128)(2,1)S(1)} %pad_maximum_fusion.4), channel_id=1, source_target_pairs={{0,6},{1,7},{2,0},{3,1},{4,2},{5,3},{6,4},{7,5},{8,14},{9,15},{10,... | collective-permute-start | bytes 1966088 | tf_op jit(solution)/shard_map/ppermute | solution.py:253
  163.4 2.4 copy-start.1
  165.7 125.4 %all-to-all-start.1 = ((bf16[32,128,640]{2,1,0:T(8,128)(2,1)}), bf16[32,128,640]{2,1,0:T(8,128)(2,1)}, u32[]{:S(2)}, u32[]{:S(2)}) async-start(bf16[32,128,640]{2,1,0:T(8,128)(2,1)} %copy-done.1), calls=%async_computation.1 | async-start | bytes 10485760 | tf_op jit(solution)/shard_map/all_to_all | solution.py:259

commit v4 on v3

v4 whole, which is shorter than its diff:
```python
import functools
import math

import jax
import jax.numpy as jnp
from jax import lax
from jax.experimental import pallas as pl
from jax.experimental.pallas import tpu as pltpu
from jax.sharding import PartitionSpec as P

HD = 128
BLK = 128
MAXDOC = 8
VMEM_BYTES = 60 * 1024 * 1024
HALO = MAXDOC - 1
CHUNKS = (2, 3, 3)
EXP2_SCALE = math.log2(math.e) / math.sqrt(HD)


def attend_kernel(doc_ref, slot_ref, order_ref, shard_ref, *refs, heads, count, base, steps, ahead, q_views):
    given, (out_ref, win_ref, held_ref, mixed_ref, kv_sems, q_sems, out_sems) = refs[:-7], refs[-7:]
    width = heads * HD
    own_ref = given[0]

    def copy_own():
        rows = (base + steps) * BLK
        return pltpu.make_async_copy(
            own_ref.at[pl.ds(0, rows), pl.ds(0, 2 * HD)], win_ref.at[pl.ds(ahead * BLK, rows)], kv_sems.at[0]
        )

    def copy_halo():
        return pltpu.make_async_copy(given[1], win_ref.at[pl.ds(0, ahead * BLK)], kv_sems.at[1])

    def copy_out(step):
        return pltpu.make_async_copy(
            mixed_ref.at[step], out_ref.at[slot_ref[base + step]], out_sems.at[step]
        )

    copy_own().start()
    if ahead:
        copy_halo().start()
    for view in range(steps):
        which, lead, row, column = q_views[view]
        source = given[which] if lead is None else given[which].at[lead]
        step = order_ref[view]
        pltpu.make_async_copy(
            source.at[pl.ds(row, BLK), pl.ds(column, width)], held_ref.at[step], q_sems.at[step]
        ).start()

    row = lax.broadcasted_iota(jnp.int32, (BLK, BLK), 0)
    column = lax.broadcasted_iota(jnp.int32, (BLK, BLK), 1)
    causal = column <= row
    copy_own().wait()
    if ahead:
        copy_halo().wait()

    def per_block(step, _):
        index = base + step
        block = shard_ref[0] * count + index
        doc = doc_ref[block]
        tiles = jnp.int32(1)
        for back in range(1, MAXDOC):
            at = jnp.maximum(block - back, 0)
            tiles += jnp.where((block >= back) & (doc_ref[at] == doc), 1, 0)
        pltpu.make_async_copy(held_ref.at[step], held_ref.at[step], q_sems.at[step]).wait()

        def with_tiles(n):
            start = pl.multiple_of((index + ahead + 1 - n) * BLK, BLK)
            keys = win_ref[pl.ds(start, n * BLK), :HD]
            values = win_ref[pl.ds(start, n * BLK), HD:]
            for head in range(heads):
                columns = slice(head * HD, (head + 1) * HD)
                scores = lax.dot_general(
                    held_ref[step, :, columns],
                    keys,
                    (((1,), (1,)), ((), ())),
                    preferred_element_type=jnp.float32,
                )
                last = jnp.where(causal, scores[:, (n - 1) * BLK :], -jnp.inf)
                if n > 1:
                    scores = jnp.concatenate([scores[:, : (n - 1) * BLK], last], axis=1)
                else:
                    scores = last
                top = jnp.max(scores, axis=1, keepdims=True)
                expo = jnp.exp2((scores - top) * EXP2_SCALE)
                total = jnp.sum(expo, axis=1, keepdims=True)
                mixed = jnp.dot(expo.astype(jnp.bfloat16), values, preferred_element_type=jnp.float32)
                mixed_ref[step, :, columns] = (mixed / total).astype(jnp.bfloat16)

        for n in range(1, MAXDOC + 1):
            pl.when(tiles == n)(functools.partial(with_tiles, n))
        copy_out(step).start()
        return 0

    lax.fori_loop(0, steps, per_block, 0)
    for step in range(steps):
        copy_out(step).wait()


def attend(own, halo, sources, q_views, order, heads, tables, count, slots, base=0, steps=None, result=None):
    doc_ids, slot, shard = tables
    steps = count if steps is None else steps
    width = heads * HD
    ahead = 0 if halo is None else HALO
    given = [own] + ([] if halo is None else [halo])
    views = [(len(given) + which if which >= 0 else 0, lead, row, column) for which, lead, row, column in q_views]
    given = given + list(sources) + ([] if result is None else [result])
    smem, anywhere = pl.BlockSpec(memory_space=pltpu.SMEM), pl.BlockSpec(memory_space=pl.ANY)
    return pl.pallas_call(
        functools.partial(
            attend_kernel, heads=heads, count=count, base=base, steps=steps, ahead=ahead, q_views=views
        ),
        in_specs=[smem] * 4 + [anywhere] * len(given),
        out_specs=pl.BlockSpec(memory_space=pl.ANY),
        out_shape=jax.ShapeDtypeStruct((slots, BLK, width), jnp.bfloat16),
        scratch_shapes=[
            pltpu.VMEM(((base + steps + ahead) * BLK, 2 * HD), jnp.bfloat16),
            pltpu.VMEM((steps, BLK, width), jnp.bfloat16),
            pltpu.VMEM((steps, BLK, width), jnp.bfloat16),
            pltpu.SemaphoreType.DMA((2,)),
            pltpu.SemaphoreType.DMA((steps,)),
            pltpu.SemaphoreType.DMA((steps,)),
        ],
        input_output_aliases={} if result is None else {4 + len(given) - 1: 0},
        compiler_params=pltpu.CompilerParams(vmem_limit_bytes=VMEM_BYTES),
        cost_estimate=pl.CostEstimate(
            flops=4 * steps * BLK * heads * HD * BLK * 4,
            bytes_accessed=4 * steps * BLK * width + 4 * (base + steps) * BLK * HD,
            transcendentals=steps * BLK * heads * BLK * 4,
        ),
        name="attend",
    )(doc_ids, slot, order, shard, *given)


def first_parts_kernel(k_ref, v_ref, q_ref, out_ref, held_ref, in_sems, out_sems, *, head_count, width):
    kv_width, q_width = k_ref.shape[1] // head_count, q_ref.shape[1] // head_count
    rows = q_ref.shape[0]

    def fetches(h):
        pieces = (
            (k_ref, h * kv_width, 0, kv_width),
            (v_ref, h * kv_width, kv_width, kv_width),
            (q_ref, h * q_width, 2 * kv_width, width),
        )
        return [
            pltpu.make_async_copy(
                ref.at[:, pl.ds(at, size)], held_ref.at[h, :, pl.ds(to, size)], in_sems.at[h, i]
            )
            for i, (ref, at, to, size) in enumerate(pieces)
        ]

    def store(h):
        return pltpu.make_async_copy(held_ref.at[h], out_ref.at[h], out_sems.at[h])

    for h in range(head_count):
        for fetch in fetches(h):
            fetch.start()
    for h in range(head_count):
        for fetch in fetches(h):
            fetch.wait()
        store(h).start()
    for h in range(head_count):
        store(h).wait()


def first_parts(key, value, query, head_count, width):
    shape = (head_count, query.shape[0], 2 * key.shape[1] // head_count + width)
    return pl.pallas_call(
        functools.partial(first_parts_kernel, head_count=head_count, width=width),
        in_specs=[pl.BlockSpec(memory_space=pl.ANY)] * 3,
        out_specs=pl.BlockSpec(memory_space=pl.ANY),
        out_shape=jax.ShapeDtypeStruct(shape, jnp.bfloat16),
        scratch_shapes=[
            pltpu.VMEM(shape, jnp.bfloat16),
            pltpu.SemaphoreType.DMA((head_count, 3)),
            pltpu.SemaphoreType.DMA((head_count,)),
        ],
        compiler_params=pltpu.CompilerParams(vmem_limit_bytes=VMEM_BYTES),
        name="first_parts",
    )(key, value, query)


def later_parts_kernel(place_ref, q_ref, *refs, chips, firsts, widths):
    sems, held_refs, out_refs = refs[-2:], refs[-2 - len(widths) : -2], refs[: -2 - len(widths)]
    core, chip = place_ref[0], place_ref[1]
    q_width = q_ref.shape[1] // (2 * chips)
    moves = []
    for chunk, (first, width) in enumerate(zip(firsts, widths)):
        for side in range(2):
            for step in range(chips):
                member = lax.rem(chip + step, chips) * 2 + lax.rem(core + side, 2)
                column = pl.multiple_of(member * q_width + first, HD)
                held = held_refs[chunk].at[side * chips + step]
                at = (chunk * 2 + side) * chips + step
                moves.append((
                    pltpu.make_async_copy(q_ref.at[:, pl.ds(column, width)], held, sems[0].at[at]),
                    pltpu.make_async_copy(held, out_refs[at], sems[1].at[at]),
                ))
    for fetch, _ in moves:
        fetch.start()
    for fetch, store in moves:
        fetch.wait()
        store.start()
    for _, store in moves:
        store.wait()


def later_parts(query, place, head_count, firsts, widths):
    rows, chips = query.shape[0], head_count // 2
    shapes = [jax.ShapeDtypeStruct((rows, width), jnp.bfloat16) for width in widths for _ in range(2 * chips)]
    outs = pl.pallas_call(
        functools.partial(later_parts_kernel, chips=chips, firsts=firsts, widths=widths),
        in_specs=[pl.BlockSpec(memory_space=pltpu.SMEM), pl.BlockSpec(memory_space=pl.ANY)],
        out_specs=[pl.BlockSpec(memory_space=pl.ANY)] * len(shapes),
        out_shape=shapes,
        scratch_shapes=[pltpu.VMEM((2 * chips, rows, width), jnp.bfloat16) for width in widths]
        + [pltpu.SemaphoreType.DMA((len(shapes),))] * 2,
        compiler_params=pltpu.CompilerParams(vmem_limit_bytes=VMEM_BYTES),
        cost_estimate=pl.CostEstimate(flops=0, bytes_accessed=4 * query.size, transcendentals=0),
        name="later_parts",
    )(place, query)
    kept = [list(outs[2 * chips * i : 2 * chips * i + chips]) for i in range(len(widths))]
    given = [list(outs[2 * chips * i + chips : 2 * chips * (i + 1)]) for i in range(len(widths))]
    return kept, given


def place_kernel(source_ref, *refs, count, first, width):
    received_ref, out_ref, held_ref, in_sems, out_sems = refs[0], refs[-4], refs[-3], refs[-2], refs[-1]

    def fetch(i):
        return pltpu.make_async_copy(received_ref.at[source_ref[i]], held_ref.at[i], in_sems.at[i])

    def store(i):
        return pltpu.make_async_copy(
            held_ref.at[i], out_ref.at[pl.ds(i * BLK, BLK), pl.ds(first, width)], out_sems.at[i]
        )

    for i in range(count):
        fetch(i).start()
    for i in range(count):
        fetch(i).wait()
        store(i).start()
    for i in range(count):
        store(i).wait()


def place(received, source, result, first, count, full_width):
    slots, _, width = received.shape
    given = [received] if result is None else [received, result]
    return pl.pallas_call(
        functools.partial(place_kernel, count=count, first=first, width=width),
        in_specs=[pl.BlockSpec(memory_space=pltpu.SMEM)] + [pl.BlockSpec(memory_space=pl.ANY)] * len(given),
        out_specs=pl.BlockSpec(memory_space=pl.ANY),
        out_shape=jax.ShapeDtypeStruct((count * BLK, full_width), jnp.bfloat16),
        scratch_shapes=[
            pltpu.VMEM((count, BLK, width), jnp.bfloat16),
            pltpu.SemaphoreType.DMA((count,)),
            pltpu.SemaphoreType.DMA((count,)),
        ],
        input_output_aliases={} if result is None else {2: 0},
        compiler_params=pltpu.CompilerParams(vmem_limit_bytes=VMEM_BYTES),
        cost_estimate=pl.CostEstimate(flops=0, bytes_accessed=4 * count * BLK * width, transcendentals=0),
        name="place",
    )(source, *given)


def shards(query, key, value, doc_ids, plan):
    head_count = lax.axis_size("head")
    shard_count = lax.axis_size("ctx")
    local_rows = query.shape[0]
    rows = head_count * local_rows
    count = rows // BLK
    per_device = local_rows // BLK
    q_width = query.shape[1] // head_count
    shard = lax.axis_index("ctx").astype(jnp.int32)
    member = lax.axis_index("head").astype(jnp.int32)
    core, chip, chips = member % 2, member // 2, head_count // 2

    widths = [heads * HD for heads in CHUNKS]
    firsts = [sum(widths[:i]) for i in range(len(widths))]
    opening = first_parts(key, value, query, head_count, widths[0])
    kept, given = later_parts(query, jnp.stack([core, chip]), head_count, firsts[1:], widths[1:])
    swap = [(h, h ^ 1) for h in range(head_count)]
    got = [[lax.ppermute(part, "head", swap) for part in parts] for parts in given]
    opening = lax.all_to_all(opening, "head", split_axis=0, concat_axis=0, tiled=True)

    index = jnp.arange(count, dtype=jnp.int32)
    own_ids = shard * count + index
    position = jnp.arange(plan.shape[0], dtype=jnp.int32)
    target = jnp.sum(
        jnp.where(plan[None, :] == own_ids[:, None], position[None, :] // count, 0), axis=1, dtype=jnp.int32
    )
    source = lax.dynamic_slice_in_dim(plan, shard * count, count) // count
    step_of, rest = index // (2 * per_device), index % (2 * per_device)
    giver = (chip - step_of + chips) % chips * 2 + (core + rest // per_device) % 2
    arrival = giver * per_device + rest % per_device

    opening, kept, got, target, source, arrival = lax.optimization_barrier(
        (opening, kept, got, target, source, arrival)
    )
    opening = opening.reshape(rows, 2 * HD + widths[0])
    halo = lax.ppermute(
        opening[rows - HALO * BLK :, : 2 * HD], "ctx", [(i, i + 1) for i in range(shard_count - 1)]
    )
    tables = (doc_ids, target, shard.reshape(1))

    result = None
    for turn, heads in enumerate(CHUNKS):
        if turn == 0:
            views = [(-1, None, i * BLK, 2 * HD) for i in range(count)]
            sent = attend(
                opening, None, [], views[HALO:], index, heads, tables, count, shard_count, HALO, count - HALO
            )
            sent = attend(
                opening, halo, [], views[:HALO], index, heads, tables, count, shard_count, 0, HALO, sent
            )
        else:
            sources = []
            for step in range(chips):
                onward = [(h, (h + 2 * step) % head_count) for h in range(head_count)]
                for part in (kept[turn - 1][step], got[turn - 1][step]):
                    sources.append(lax.ppermute(part, "head", onward) if step else part)
            views = [(i // per_device, None, i % per_device * BLK, 0) for i in range(count)]
            sent = attend(opening, halo, sources, views, arrival, heads, tables, count, shard_count)
        received = lax.all_to_all(sent, "ctx", split_axis=0, concat_axis=0, tiled=True)
        result = place(received, source, result, firsts[turn], count, q_width)
    return result


def solution(mesh):
    return jax.shard_map(
        shards,
        mesh=mesh,
        in_specs=(
            P(("ctx", "head"), None),
            P(("ctx", "head"), None),
            P(("ctx", "head"), None),
            P(),
            P(),
        ),
        out_specs=P("ctx", "head"),
        check_vma=False,
    )
```

time: 299 us -> 285 us (0.953)
  waiting for transfers between devices: 165 us -> 149 us
  starting transfers between devices: 47.3 us -> 51.4 us
    ppermute x8 -> x20, waiting for transfers between devices: 42.1 us -> 27 us  [the longest x12 26.5 us: shards(): sources.append(lax.ppermute(part, 'head', onward) if step else part)]
    all_to_all x1, waiting for transfers between devices: 8.75 us -> 16.9 us  [shards(): lax.all_to_all(opening, 'head', split_axis=0, concat_axis=0, tiled=True)]
    ppermute x8 -> x20, starting transfers between devices: 8.35 us -> 16.3 us  [the longest x12 14.1 us: shards(): sources.append(lax.ppermute(part, 'head', onward) if step else part)]
    all_to_all x3, waiting for transfers between devices: 111 us -> 105 us  [shards(): lax.all_to_all(sent, 'ctx', split_axis=0, concat_axis=0, tiled=True)]
    pallas_call x2, Pallas kernels: 12.8 us -> 6.56 us  [the longest x1 3.92 us: later_parts(): pl.pallas_call(functools.partial(later_parts_kernel, chips=chips, firsts=...]
    pallas_call x4, Pallas kernels: 51 us -> 57 us  [attend(): pl.pallas_call(functools.partial(attend_kernel, heads=heads, count=count,...]
    all_to_all x3, starting transfers between devices: 30.3 us -> 26.4 us  [shards(): lax.all_to_all(sent, 'ctx', split_axis=0, concat_axis=0, tiled=True)]
    slice x4 -> x0, local copies, waits for them, and re-layouts: 3.87 us -> none  [shards(): piece = jnp.stack([kept[turn - 1][step], got[turn - 1][step]])]
  transfers between devices with their start and end apart: 13 -> 25, of which waited for: 10 -> 14; matrix products, arithmetic and copies ran while one was open for 2% -> 1% of each run, Pallas kernels for 20% -> 21%
where the time goes in v4:
time: 285 us; the launch traced here: 281 us
  waiting for transfers between devices  149 us (52%)
  Pallas kernels  72.5 us (25%)
  starting transfers between devices  51.4 us (18%)
  local copies, waits for them, and re-layouts  5.79 us (2%)
    all_to_all x3, waiting for transfers between devices, shards(): lax.all_to_all(sent, 'ctx', split_axis=0, concat_axis=0, tiled=True)  105 us
    pallas_call x4, Pallas kernels, attend(): pl.pallas_call(functools.partial(attend_kernel, heads=heads, count=count,...  57 us
    ppermute x12, waiting for transfers between devices, shards(): sources.append(lax.ppermute(part, 'head', onward) if step else part)  26.5 us
    all_to_all x3, starting transfers between devices, shards(): lax.all_to_all(sent, 'ctx', split_axis=0, concat_axis=0, tiled=True)  26.4 us
    all_to_all x1, waiting for transfers between devices, shards(): lax.all_to_all(opening, 'head', split_axis=0, concat_axis=0, tiled=True)  16.9 us
    ppermute x12, starting transfers between devices, shards(): sources.append(lax.ppermute(part, 'head', onward) if step else part)  14.1 us
    pallas_call x3, Pallas kernels, place(): pl.pallas_call(functools.partial(place_kernel, count=count, first=first,...  8.94 us
  transfers between devices with their start and end apart: 25, of which 14 were waited for; matrix products, arithmetic and copies ran while one was open for 1% of the time, Pallas kernels for 21%

profile of v4, /device:TPU:33, one launch (start us, length us, event | category | flops | bytes accessed | tf_op | source)
XLA Modules:
  0.0 280.8 jit_solution(6850155624269804485)
XLA Ops:
  0.0 2.6 first_parts.1
  2.6 5.2 %all-to-all-start = ((bf16[8,256,512]{2,1,0:T(8,128)(2,1)}), bf16[8,256,512]{2,1,0:T(8,128)(2,1)S(1)}, u32[]{:S(2)}, u32[]{:S(2)}) async-start(bf16[8,256,512]{2,1,0:T(8,128)(2,1)} %first_parts.1), calls=%async_computation | async-start | bytes 4194304 | tf_op jit(solution)/shard_map/all_to_all | solution.py:285
  7.8 0.6 pad_add_fusion.place_ref
  8.4 3.9 %later_parts.1 = (bf16[256,384]{1,0:T(8,128)(2,1)}, bf16[256,384]{1,0:T(8,128)(2,1)}, bf16[256,384]{1,0:T(8,128)(2,1)}, bf16[256,384]{1,0:T(8,128)(2,1)}, bf16[2...) custom-call(s32[2]{0:T(128)} %pad_add_fusion.place_ref, ...), custom_call_target="tpu_custom_call" | custom-call | bytes 8388608 | tf_op jit(solution)/shard_map/later_parts/pallas_call | solution.py:211
  12.5 0.5 collective-permute-start.1
  13.1 0.4 collective-permute-start.3
  13.6 0.7 and_select_fusion.6
  14.3 0.5 collective-permute-start.5
  14.9 0.7 copy-done.22
  15.6 0.4 collective-permute-start.7
  16.0 0.8 select_reduce_fusion.slot_ref
  16.8 0.5 collective-permute-done.7
  17.3 16.9 %all-to-all-done = bf16[8,256,512]{2,1,0:T(8,128)(2,1)S(1)} async-done(((bf16[8,256,512]{2,1,0:T(8,128)(2,1)}), bf16[8,256,512]{2,1,0:T(8,128)(2,1)S(1)}, u32[]{:S(2)}, u32[]{:S(2)}) %all-to-all-start) | async-done | bytes 2097184 | tf_op jit(solution)/shard_map/all_to_all | solution.py:285
  34.2 3.5 %collective-permute-start.8 = (bf16[896,256]{1,0:T(8,128)(2,1)S(1)}, bf16[896,256]{1,0:T(8,128)(2,1)S(1)}, u32[]{:S(2)}, u32[]{:S(2)}) collective-permute-start(bf16[896,256]{1,0:T(8,128)(2,1)S(1)} %slice.4), channel_id=1, source_target_pairs={{0,8},{8,16},{16,24},{24,32},{32,40},{40,48},{48,56},{56,64},{64,7... | collective-permute-start | bytes 1376264 | tf_op jit(solution)/shard_map/ppermute | solution.py:302
  37.7 0.5 iota.24.order_ref
  38.2 10.1 %attend.6.refs_2_ = bf16[32,128,256]{2,1,0:T(8,128)(2,1)} custom-call(s32[512]{0:T(512)} %doc_ref.7, s32[16]{0:T(128)} %select_reduce_fusion.slot_ref, s32[16]{0:T(128)} %iota.24.order_ref, s32[1]{0:T(128)} %bitcast.2.shard_ref, bf16[2048,512]{1,0:T(8,128)(2,1)} %bitcast.5), custom_call_target="tpu_custom_call" | custom-call | flops 603979776 | bytes 2228224 | tf_op jit(solution)/shard_map/attend/pallas_call | solution.py:109
  48.3 0.6 iota.23.order_ref
  49.1 7.9 %attend.7 = bf16[32,128,256]{2,1,0:T(8,128)(2,1)} custom-call(s32[512]{0:T(512)} %doc_ref.7, s32[16]{0:T(128)} %select_reduce_fusion.slot_ref, s32[16]{0:T(128)} %iota.23.order_ref, s32[1]{0:T(128)} %bitcast.2.shard_ref, bf16[2048,512]{1,0:T(8,128)(2,1)} %bitcast.6, bf16[896,256]{1,0:T(8,128)(2,1)} %copy-done.3, ...), custom_call_target="tpu_custom_call", output_to_operand_aliasing={{}: (6, {})} | custom-call | flops 469762048 | bytes 1376256 | tf_op jit(solution)/shard_map/attend/pallas_call | solution.py:109
  57.1 11.6 %all-to-all-start.3 = ((bf16[32,128,256]{2,1,0:T(8,128)(2,1)}), bf16[32,128,256]{2,1,0:T(8,128)(2,1)S(1)}, u32[]{:S(2)}, u32[]{:S(2)}) async-start(bf16[32,128,256]{2,1,0:T(8,128)(2,1)} %attend.7), calls=%async_computation.3 | async-start | bytes 4194304 | tf_op jit(solution)/shard_map/all_to_all | solution.py:325
  68.7 0.4 collective-permute-start.15
  69.2 3.5 %collective-permute-start.17 = (bf16[256,384]{1,0:T(8,128)(2,1)S(1)}, bf16[256,384]{1,0:T(8,128)(2,1)S(1)}, u32[]{:S(2)}, u32[]{:S(2)}) collective-permute-start(bf16[256,384]{1,0:T(8,128)(2,1)S(1)} %copy-done.20), channel_id=1, source_target_pairs={{0,4},{1,5},{2,6},{3,7},{4,0},{5,1},{6,2},{7,3},{8,12},{9,13},{10,... | collective-permute-start | bytes 589832 | tf_op jit(solution)/shard_map/ppermute | solution.py:322
  72.7 2.0 collective-permute-start.19
  74.7 1.2 collective-permute-start.20
  75.9 3.2 %collective-permute-done.16.refs_5_ = bf16[256,384]{1,0:T(8,128)(2,1)S(1)} collective-permute-done((bf16[256,384]{1,0:T(8,128)(2,1)}, bf16[256,384]{1,0:T(8,128)(2,1)S(1)}, u32[]{:S(2)}, u32[]{:S(2)}) %collective-permute-start.16) | collective-permute-done | bytes 196640 | tf_op jit(solution)/shard_map/ppermute | solution.py:322
  79.1 3.0 %collective-permute-done.17.refs_6_ = bf16[256,384]{1,0:T(8,128)(2,1)S(1)} collective-permute-done((bf16[256,384]{1,0:T(8,128)(2,1)S(1)}, bf16[256,384]{1,0:T(8,128)(2,1)S(1)}, u32[]{:S(2)}, u32[]{:S(2)}) %collective-permute-start.17) | collective-permute-done | bytes 196640 | tf_op jit(solution)/shard_map/ppermute | solution.py:322
  82.1 4.3 %collective-permute-done.18.refs_7_ = bf16[256,384]{1,0:T(8,128)(2,1)S(1)} collective-permute-done((bf16[256,384]{1,0:T(8,128)(2,1)}, bf16[256,384]{1,0:T(8,128)(2,1)S(1)}, u32[]{:S(2)}, u32[]{:S(2)}) %collective-permute-start.18) | collective-permute-done | bytes 196640 | tf_op jit(solution)/shard_map/ppermute | solution.py:322
  86.4 2.3 collective-permute-done.20.refs_9_
  88.7 0.7 copy-done.15
  89.3 19.5 %attend.5 = bf16[32,128,384]{2,1,0:T(8,128)(2,1)} custom-call(s32[512]{0:T(512)} %doc_ref.7, s32[16]{0:T(128)} %select_reduce_fusion.slot_ref, s32[16]{0:T(128)} %get-tuple-element.59.order_ref, s32[1]{0:T(128)} %bitcast.2.shard_ref, bf16[2048,512]{1,0:T(8,128)(2,1)} %bitcast.7, bf16[896,256]{1,0:T(8,128)(2,1)} %copy-done.3, ...), custom_call_target="tpu_custom_call" | custom-call | flops 1610612736 | bytes 4194304 | tf_op jit(solution)/shard_map/attend/pallas_call | solution.py:109
  108.9 8.9 %all-to-all-done.3.refs_0_ = bf16[32,128,256]{2,1,0:T(8,128)(2,1)S(1)} async-done(((bf16[32,128,256]{2,1,0:T(8,128)(2,1)}), bf16[32,128,256]{2,1,0:T(8,128)(2,1)S(1)}, u32[]{:S(2)}, u32[]{:S(2)}) %all-to-all-start.3) | async-done | bytes 2097184 | tf_op jit(solution)/shard_map/all_to_all | solution.py:325
  117.8 1.3 copy-done.2
  119.1 6.5 %all-to-all-start.2 = ((bf16[32,128,384]{2,1,0:T(8,128)(2,1)}), bf16[32,128,384]{2,1,0:T(8,128)(2,1)S(1)}, u32[]{:S(2)}, u32[]{:S(2)}) async-start(bf16[32,128,384]{2,1,0:T(8,128)(2,1)} %attend.5), calls=%async_computation.2 | async-start | bytes 6291456 | tf_op jit(solution)/shard_map/all_to_all | solution.py:325
  125.6 0.4 collective-permute-start.9
  126.1 3.4 %collective-permute-start.11 = (bf16[256,384]{1,0:T(8,128)(2,1)}, bf16[256,384]{1,0:T(8,128)(2,1)S(1)}, u32[]{:S(2)}, u32[]{:S(2)}) collective-permute-start(bf16[256,384]{1,0:T(8,128)(2,1)} %get-tuple-element.65), channel_id=1, source_target_pairs={{0,4},{1,5},{2,6},{3,7},{4,0},{5,1},{6,2},{7,3},{8,12},{9,13},{10,... | collective-permute-start | bytes 589832 | tf_op jit(solution)/shard_map/ppermute | solution.py:322
  129.6 2.0 collective-permute-start.13
  131.9 0.9 collective-permute-start.14
  132.8 3.7 %collective-permute-done.10.refs_5_ = bf16[256,384]{1,0:T(8,128)(2,1)S(1)} collective-permute-done((bf16[256,384]{1,0:T(8,128)(2,1)}, bf16[256,384]{1,0:T(8,128)(2,1)S(1)}, u32[]{:S(2)}, u32[]{:S(2)}) %collective-permute-start.10) | collective-permute-done | bytes 196640 | tf_op jit(solution)/shard_map/ppermute | solution.py:322
  136.5 3.0 %collective-permute-done.11.refs_6_ = bf16[256,384]{1,0:T(8,128)(2,1)S(1)} collective-permute-done((bf16[256,384]{1,0:T(8,128)(2,1)}, bf16[256,384]{1,0:T(8,128)(2,1)S(1)}, u32[]{:S(2)}, u32[]{:S(2)}) %collective-permute-start.11) | collective-permute-done | bytes 196640 | tf_op jit(solution)/shard_map/ppermute | solution.py:322
  139.5 4.3 %collective-permute-done.12.refs_7_ = bf16[256,384]{1,0:T(8,128)(2,1)S(1)} collective-permute-done((bf16[256,384]{1,0:T(8,128)(2,1)}, bf16[256,384]{1,0:T(8,128)(2,1)S(1)}, u32[]{:S(2)}, u32[]{:S(2)}) %collective-permute-start.12) | collective-permute-done | bytes 196640 | tf_op jit(solution)/shard_map/ppermute | solution.py:322
  143.7 2.5 collective-permute-done.14.refs_9_
  146.3 19.5 %attend.4 = bf16[32,128,384]{2,1,0:T(8,128)(2,1)} custom-call(s32[512]{0:T(512)} %doc_ref.7, s32[16]{0:T(128)} %select_reduce_fusion.slot_ref, s32[16]{0:T(128)} %get-tuple-element.59.order_ref, s32[1]{0:T(128)} %bitcast.2.shard_ref, bf16[2048,512]{1,0:T(8,128)(2,1)} %bitcast.8, bf16[896,256]{1,0:T(8,128)(2,1)} %copy-done.3, ...), custom_call_target="tpu_custom_call" | custom-call | flops 1610612736 | bytes 4194304 | tf_op jit(solution)/shard_map/attend/pallas_call | solution.py:109
  165.8 30.6 %all-to-all-done.2.refs_0_ = bf16[32,128,384]{2,1,0:T(8,128)(2,1)S(1)} async-done(((bf16[32,128,384]{2,1,0:T(8,128)(2,1)}), bf16[32,128,384]{2,1,0:T(8,128)(2,1)S(1)}, u32[]{:S(2)}, u32[]{:S(2)}) %all-to-all-start.2) | async-done | bytes 3145760 | tf_op jit(solution)/shard_map/all_to_all | solution.py:325
  196.4 1.7 copy-done.1
  198.1 8.2 %all-to-all-start.1 = ((bf16[32,128,384]{2,1,0:T(8,128)(2,1)}), bf16[32,128,384]{2,1,0:T(8,128)(2,1)}, u32[]{:S(2)}, u32[]{:S(2)}) async-start(bf16[32,128,384]{2,1,0:T(8,128)(2,1)} %attend.4), calls=%async_computation.1 | async-start | bytes 6291456 | tf_op jit(solution)/shard_map/all_to_all | solution.py:325
  206.4 2.8 %place.3.refs_1_ = bf16[2048,1024]{1,0:T(8,128)(2,1)} custom-call(s32[16]{0:T(128)} %get-tuple-element.57.source_ref, bf16[32,128,256]{2,1,0:T(8,128)(2,1)} %copy-done.2), custom_call_target="tpu_custom_call" | custom-call | bytes 2097152 | tf_op jit(solution)/shard_map/place/pallas_call | solution.py:250
  209.2 3.1 %place.4.refs_1_ = bf16[2048,1024]{1,0:T(8,128)(2,1)} custom-call(s32[16]{0:T(128)} %get-tuple-element.57.source_ref, bf16[32,128,384]{2,1,0:T(8,128)(2,1)} %copy-done.1, bf16[2048,1024]{1,0:T(8,128)(2,1)} %place.3.refs_1_), custom_call_target="tpu_custom_call", output_to_operand_aliasing={{}: (2, {})} | custom-call | bytes 3145728 | tf_op jit(solution)/shard_map/place/pallas_call | solution.py:250
  212.3 65.3 %all-to-all-done.1.refs_0_ = bf16[32,128,384]{2,1,0:T(8,128)(2,1)} async-done(((bf16[32,128,384]{2,1,0:T(8,128)(2,1)}), bf16[32,128,384]{2,1,0:T(8,128)(2,1)}, u32[]{:S(2)}, u32[]{:S(2)}) %all-to-all-start.1) | async-done | bytes 3145760 | tf_op jit(solution)/shard_map/all_to_all | solution.py:325
  277.5 3.1 %place.5 = bf16[2048,1024]{1,0:T(8,128)(2,1)} custom-call(s32[16]{0:T(128)} %get-tuple-element.57.source_ref, bf16[32,128,384]{2,1,0:T(8,128)(2,1)} %all-to-all-done.1.refs_0_, bf16[2048,1024]{1,0:T(8,128)(2,1)} %place.4.refs_1_), custom_call_target="tpu_custom_call", output_to_operand_aliasing={{}: (2, {})} | custom-call | bytes 3145728 | tf_op jit(solution)/shard_map/place/pallas_call | solution.py:250
  (65 shorter events, 1.5 us)
Async XLA Ops:
  2.6 31.5 %all-to-all-start = ((bf16[8,256,512]{2,1,0:T(8,128)(2,1)}), bf16[8,256,512]{2,1,0:T(8,128)(2,1)S(1)}, u32[]{:S(2)}, u32[]{:S(2)}) async-start(bf16[8,256,512]{2,1,0:T(8,128)(2,1)} %first_parts.1), calls=%async_computation | async-start | bytes 4194304 | tf_op jit(solution)/shard_map/all_to_all | solution.py:285
  7.8 5.8 %copy-start.16 = (s32[512]{0:T(512)S(1)}, s32[512]{0:T(512)}, u32[]{:S(2)}) copy-start(s32[512]{0:T(512)} %param.9) | copy-start | bytes 6148
  12.4 1.9 collective-permute-start
  12.5 2.3 collective-permute-start.1
  13.0 1.9 collective-permute-start.2
  13.1 3.7 %collective-permute-start.3 = (bf16[256,384]{1,0:T(8,128)(2,1)}, bf16[256,384]{1,0:T(8,128)(2,1)S(1)}, u32[]{:S(2)}, u32[]{:S(2)}) collective-permute-start(bf16[256,384]{1,0:T(8,128)(2,1)} %get-tuple-element.52), channel_id=1, source_target_pairs={{0,1},{1,0},{2,3},{3,2},{4,5},{5,4},{6,7},{7,6},{8,9},{9,8},{10,11... | collective-permute-start | bytes 589832 | tf_op jit(solution)/shard_map/ppermute | solution.py:284
  13.5 3.3 %collective-permute-start.4 = (bf16[256,384]{1,0:T(8,128)(2,1)}, bf16[256,384]{1,0:T(8,128)(2,1)S(1)}, u32[]{:S(2)}, u32[]{:S(2)}) collective-permute-start(bf16[256,384]{1,0:T(8,128)(2,1)} %get-tuple-element.53), channel_id=1, source_target_pairs={{0,1},{1,0},{2,3},{3,2},{4,5},{5,4},{6,7},{7,6},{8,9},{9,8},{10,11... | collective-permute-start | bytes 589832 | tf_op jit(solution)/shard_map/ppermute | solution.py:284
  14.3 42.8 %copy-start.5 = (bf16[256,384]{1,0:T(8,128)(2,1)}, bf16[256,384]{1,0:T(8,128)(2,1)S(1)}, u32[]{:S(2)}) copy-start(bf16[256,384]{1,0:T(8,128)(2,1)S(1)} %collective-permute-done.refs_3_) | copy-start | bytes 589828
  14.3 2.5 collective-permute-start.5
  14.8 2.0 collective-permute-start.6
  14.9 0.7 copy-start.22
  15.6 1.7 collective-permute-start.7
  16.8 17.4 %copy-start.21 = (bf16[256,384]{1,0:T(8,128)(2,1)}, bf16[256,384]{1,0:T(8,128)(2,1)S(1)}, u32[]{:S(2)}) copy-start(bf16[256,384]{1,0:T(8,128)(2,1)S(1)} %collective-permute-done.3) | copy-start | bytes 589828
  16.8 40.3 %copy-start.4 = (bf16[256,384]{1,0:T(8,128)(2,1)}, bf16[256,384]{1,0:T(8,128)(2,1)S(1)}, u32[]{:S(2)}) copy-start(bf16[256,384]{1,0:T(8,128)(2,1)S(1)} %collective-permute-done.4.refs_3_) | copy-start | bytes 589828
  16.8 32.1 %copy-start.18 = (bf16[256,384]{1,0:T(8,128)(2,1)}, bf16[256,384]{1,0:T(8,128)(2,1)S(1)}, u32[]{:S(2)}) copy-start(bf16[256,384]{1,0:T(8,128)(2,1)S(1)} %collective-permute-done.6) | copy-start | bytes 589828
  17.3 16.9 %copy-start.19 = (bf16[256,384]{1,0:T(8,128)(2,1)}, bf16[256,384]{1,0:T(8,128)(2,1)S(1)}, u32[]{:S(2)}) copy-start(bf16[256,384]{1,0:T(8,128)(2,1)S(1)} %collective-permute-done.7) | copy-start | bytes 589828
  34.1 4.1 %copy-start = (bf16[8,256,512]{2,1,0:T(8,128)(2,1)}, bf16[8,256,512]{2,1,0:T(8,128)(2,1)S(1)}, u32[]{:S(2)}) copy-start(bf16[8,256,512]{2,1,0:T(8,128)(2,1)S(1)} %all-to-all-done) | copy-start | bytes 6291460
  34.2 14.1 %collective-permute-start.8 = (bf16[896,256]{1,0:T(8,128)(2,1)S(1)}, bf16[896,256]{1,0:T(8,128)(2,1)S(1)}, u32[]{:S(2)}, u32[]{:S(2)}) collective-permute-start(bf16[896,256]{1,0:T(8,128)(2,1)S(1)} %slice.4), channel_id=1, source_target_pairs={{0,8},{8,16},{16,24},{24,32},{32,40},{40,48},{48,56},{56,64},{64,7... | collective-permute-start | bytes 1376264 | tf_op jit(solution)/shard_map/ppermute | solution.py:302
  48.3 0.8 copy-start.3
  57.0 12.1 %copy-start.20 = (bf16[256,384]{1,0:T(8,128)(2,1)S(1)}, bf16[256,384]{1,0:T(8,128)(2,1)}, u32[]{:S(2)}) copy-start(bf16[256,384]{1,0:T(8,128)(2,1)} %get-tuple-element.73) | copy-start | bytes 589828
  57.1 15.6 %copy-start.17 = (bf16[256,384]{1,0:T(8,128)(2,1)S(1)}, bf16[256,384]{1,0:T(8,128)(2,1)}, u32[]{:S(2)}) copy-start(bf16[256,384]{1,0:T(8,128)(2,1)} %get-tuple-element.75) | copy-start | bytes 589828
  57.1 60.7 %all-to-all-start.3 = ((bf16[32,128,256]{2,1,0:T(8,128)(2,1)}), bf16[32,128,256]{2,1,0:T(8,128)(2,1)S(1)}, u32[]{:S(2)}, u32[]{:S(2)}) async-start(bf16[32,128,256]{2,1,0:T(8,128)(2,1)} %attend.7), calls=%async_computation.3 | async-start | bytes 4194304 | tf_op jit(solution)/shard_map/all_to_all | solution.py:325
  68.7 6.0 %collective-permute-start.15 = (bf16[256,384]{1,0:T(8,128)(2,1)}, bf16[256,384]{1,0:T(8,128)(2,1)S(1)}, u32[]{:S(2)}, u32[]{:S(2)}) collective-permute-start(bf16[256,384]{1,0:T(8,128)(2,1)} %get-tuple-element.71), channel_id=1, source_target_pairs={{0,2},{1,3},{2,4},{3,5},{4,6},{5,7},{6,0},{7,1},{8,10},{9,11},{10,... | collective-permute-start | bytes 589832 | tf_op jit(solution)/shard_map/ppermute | solution.py:322
  69.1 10.0 %collective-permute-start.16 = (bf16[256,384]{1,0:T(8,128)(2,1)}, bf16[256,384]{1,0:T(8,128)(2,1)S(1)}, u32[]{:S(2)}, u32[]{:S(2)}) collective-permute-start(bf16[256,384]{1,0:T(8,128)(2,1)} %collective-permute-done.1), channel_id=1, source_target_pairs={{0,2},{1,3},{2,4},{3,5},{4,6},{5,7},{6,0},{7,1},{8,10},{9,11},{10,... | collective-permute-start | bytes 589832 | tf_op jit(solution)/shard_map/ppermute | solution.py:322
  69.2 12.9 %collective-permute-start.17 = (bf16[256,384]{1,0:T(8,128)(2,1)S(1)}, bf16[256,384]{1,0:T(8,128)(2,1)S(1)}, u32[]{:S(2)}, u32[]{:S(2)}) collective-permute-start(bf16[256,384]{1,0:T(8,128)(2,1)S(1)} %copy-done.20), channel_id=1, source_target_pairs={{0,4},{1,5},{2,6},{3,7},{4,0},{5,1},{6,2},{7,3},{8,12},{9,13},{10,... | collective-permute-start | bytes 589832 | tf_op jit(solution)/shard_map/ppermute | solution.py:322
  72.7 13.7 %collective-permute-start.18 = (bf16[256,384]{1,0:T(8,128)(2,1)}, bf16[256,384]{1,0:T(8,128)(2,1)S(1)}, u32[]{:S(2)}, u32[]{:S(2)}) collective-permute-start(bf16[256,384]{1,0:T(8,128)(2,1)} %copy-done.22), channel_id=1, source_target_pairs={{0,4},{1,5},{2,6},{3,7},{4,0},{5,1},{6,2},{7,3},{8,12},{9,13},{10,... | collective-permute-start | bytes 589832 | tf_op jit(solution)/shard_map/ppermute | solution.py:322
  72.7 13.7 %collective-permute-start.19 = (bf16[256,384]{1,0:T(8,128)(2,1)S(1)}, bf16[256,384]{1,0:T(8,128)(2,1)S(1)}, u32[]{:S(2)}, u32[]{:S(2)}) collective-permute-start(bf16[256,384]{1,0:T(8,128)(2,1)S(1)} %copy-done.17), channel_id=1, source_target_pairs={{0,6},{1,7},{2,0},{3,1},{4,2},{5,3},{6,4},{7,5},{8,14},{9,15},{10,... | collective-permute-start | bytes 589832 | tf_op jit(solution)/shard_map/ppermute | solution.py:322
  74.7 13.9 %copy-start.8 = (bf16[256,384]{1,0:T(8,128)(2,1)}, bf16[256,384]{1,0:T(8,128)(2,1)S(1)}, u32[]{:S(2)}) copy-start(bf16[256,384]{1,0:T(8,128)(2,1)S(1)} %collective-permute-done.15.refs_4_) | copy-start | bytes 589828
  74.7 13.9 %collective-permute-start.20 = (bf16[256,384]{1,0:T(8,128)(2,1)}, bf16[256,384]{1,0:T(8,128)(2,1)S(1)}, u32[]{:S(2)}, u32[]{:S(2)}) collective-permute-start(bf16[256,384]{1,0:T(8,128)(2,1)} %copy-done.21), channel_id=1, source_target_pairs={{0,6},{1,7},{2,0},{3,1},{4,2},{5,3},{6,4},{7,5},{8,14},{9,15},{10,... | collective-permute-start | bytes 589832 | tf_op jit(solution)/shard_map/ppermute | solution.py:322
  79.1 9.5 %copy-start.10 = (bf16[256,384]{1,0:T(8,128)(2,1)}, bf16[256,384]{1,0:T(8,128)(2,1)S(1)}, u32[]{:S(2)}) copy-start(bf16[256,384]{1,0:T(8,128)(2,1)S(1)} %collective-permute-done.16.refs_5_) | copy-start | bytes 589828
  82.1 6.5 %copy-start.12 = (bf16[256,384]{1,0:T(8,128)(2,1)}, bf16[256,384]{1,0:T(8,128)(2,1)S(1)}, u32[]{:S(2)}) copy-start(bf16[256,384]{1,0:T(8,128)(2,1)S(1)} %collective-permute-done.17.refs_6_) | copy-start | bytes 589828
  86.4 2.3 copy-start.13
  86.4 2.3 copy-start.14
  88.7 0.7 copy-start.15
  117.8 1.3 copy-start.2
  119.1 77.4 %all-to-all-start.2 = ((bf16[32,128,384]{2,1,0:T(8,128)(2,1)}), bf16[32,128,384]{2,1,0:T(8,128)(2,1)S(1)}, u32[]{:S(2)}, u32[]{:S(2)}) async-start(bf16[32,128,384]{2,1,0:T(8,128)(2,1)} %attend.5), calls=%async_computation.2 | async-start | bytes 6291456 | tf_op jit(solution)/shard_map/all_to_all | solution.py:325
  125.6 6.3 %collective-permute-start.9 = (bf16[256,384]{1,0:T(8,128)(2,1)}, bf16[256,384]{1,0:T(8,128)(2,1)S(1)}, u32[]{:S(2)}, u32[]{:S(2)}) collective-permute-start(bf16[256,384]{1,0:T(8,128)(2,1)} %get-tuple-element.63), channel_id=1, source_target_pairs={{0,2},{1,3},{2,4},{3,5},{4,6},{5,7},{6,0},{7,1},{8,10},{9,11},{10,... | collective-permute-start | bytes 589832 | tf_op jit(solution)/shard_map/ppermute | solution.py:322
  125.9 10.5 %collective-permute-start.10 = (bf16[256,384]{1,0:T(8,128)(2,1)}, bf16[256,384]{1,0:T(8,128)(2,1)S(1)}, u32[]{:S(2)}, u32[]{:S(2)}) collective-permute-start(bf16[256,384]{1,0:T(8,128)(2,1)} %collective-permute-done.5), channel_id=1, source_target_pairs={{0,2},{1,3},{2,4},{3,5},{4,6},{5,7},{6,0},{7,1},{8,10},{9,11},{10,... | collective-permute-start | bytes 589832 | tf_op jit(solution)/shard_map/ppermute | solution.py:322
  126.1 13.3 %collective-permute-start.11 = (bf16[256,384]{1,0:T(8,128)(2,1)}, bf16[256,384]{1,0:T(8,128)(2,1)S(1)}, u32[]{:S(2)}, u32[]{:S(2)}) collective-permute-start(bf16[256,384]{1,0:T(8,128)(2,1)} %get-tuple-element.65), channel_id=1, source_target_pairs={{0,4},{1,5},{2,6},{3,7},{4,0},{5,1},{6,2},{7,3},{8,12},{9,13},{10,... | collective-permute-start | bytes 589832 | tf_op jit(solution)/shard_map/ppermute | solution.py:322
  129.5 14.2 %collective-permute-start.12 = (bf16[256,384]{1,0:T(8,128)(2,1)}, bf16[256,384]{1,0:T(8,128)(2,1)S(1)}, u32[]{:S(2)}, u32[]{:S(2)}) collective-permute-start(bf16[256,384]{1,0:T(8,128)(2,1)} %copy-done.18), channel_id=1, source_target_pairs={{0,4},{1,5},{2,6},{3,7},{4,0},{5,1},{6,2},{7,3},{8,12},{9,13},{10,... | collective-permute-start | bytes 589832 | tf_op jit(solution)/shard_map/ppermute | solution.py:322
  129.6 14.2 %collective-permute-start.13 = (bf16[256,384]{1,0:T(8,128)(2,1)}, bf16[256,384]{1,0:T(8,128)(2,1)}, u32[]{:S(2)}, u32[]{:S(2)}) collective-permute-start(bf16[256,384]{1,0:T(8,128)(2,1)} %get-tuple-element.67), channel_id=1, source_target_pairs={{0,6},{1,7},{2,0},{3,1},{4,2},{5,3},{6,4},{7,5},{8,14},{9,15},{10,... | collective-permute-start | bytes 589832 | tf_op jit(solution)/shard_map/ppermute | solution.py:322
  131.9 14.4 %copy-start.6 = (bf16[256,384]{1,0:T(8,128)(2,1)}, bf16[256,384]{1,0:T(8,128)(2,1)S(1)}, u32[]{:S(2)}) copy-start(bf16[256,384]{1,0:T(8,128)(2,1)S(1)} %collective-permute-done.9.refs_4_) | copy-start | bytes 589828
  131.9 14.4 %collective-permute-start.14 = (bf16[256,384]{1,0:T(8,128)(2,1)}, bf16[256,384]{1,0:T(8,128)(2,1)}, u32[]{:S(2)}, u32[]{:S(2)}) collective-permute-start(bf16[256,384]{1,0:T(8,128)(2,1)} %copy-done.19), channel_id=1, source_target_pairs={{0,6},{1,7},{2,0},{3,1},{4,2},{5,3},{6,4},{7,5},{8,14},{9,15},{10,... | collective-permute-start | bytes 589832 | tf_op jit(solution)/shard_map/ppermute | solution.py:322
  136.5 9.8 %copy-start.7 = (bf16[256,384]{1,0:T(8,128)(2,1)}, bf16[256,384]{1,0:T(8,128)(2,1)S(1)}, u32[]{:S(2)}) copy-start(bf16[256,384]{1,0:T(8,128)(2,1)S(1)} %collective-permute-done.10.refs_5_) | copy-start | bytes 589828
  139.5 6.8 %copy-start.9 = (bf16[256,384]{1,0:T(8,128)(2,1)}, bf16[256,384]{1,0:T(8,128)(2,1)S(1)}, u32[]{:S(2)}) copy-start(bf16[256,384]{1,0:T(8,128)(2,1)S(1)} %collective-permute-done.11.refs_6_) | copy-start | bytes 589828
  143.7 2.6 copy-start.11
  196.4 1.7 copy-start.1
  198.1 79.4 %all-to-all-start.1 = ((bf16[32,128,384]{2,1,0:T(8,128)(2,1)}), bf16[32,128,384]{2,1,0:T(8,128)(2,1)}, u32[]{:S(2)}, u32[]{:S(2)}) async-start(bf16[32,128,384]{2,1,0:T(8,128)(2,1)} %attend.4), calls=%async_computation.1 | async-start | bytes 6291456 | tf_op jit(solution)/shard_map/all_to_all | solution.py:325
